TPU v7x, 32 devices: a whole 2x2x4 slice. The times are simulated.
32 devices in a mesh: ax: 2 (over x), az: 4 (over z), rad: 4 (over y, core).
Axes of the slice: x: 2, y: 2, z: 4, core: 2. Of those that a mesh axis runs over, the one named last changes fastest.
Arguments:
- velocity: float32 [512, 64, 512], P('rad', 'az', 'ax'), may hold values from -4 to 4
- radial_courant: bfloat16 [512, 64, 512], P('rad', 'az', 'ax'), may hold values from -0.5 to 0.5
- axial_courant: bfloat16 [512, 64, 512], P('rad', 'az', 'ax'), may hold values from -0.5 to 0.5
- radial_diffusion: float32 [512], P('rad'), may hold values from 2048 to 8192
Outputs:
- advanced: float32 [512, 64, 512], P('rad', 'az', 'ax')
All inputs are finite; a program needn't handle non-finite values.
Results may differ from a plain program's by a relative error of at most 0.0009.
Values sent between devices are 32-bit elements; how exact they have to be, the bound alone decides.
A program may use at most 64 MiB of HBM per device.

v0:
```python
import functools

import jax
import jax.numpy as jnp
from jax import lax
from jax.experimental import pallas as pl
from jax.experimental.pallas import tpu as pltpu
from jax.sharding import PartitionSpec as P

NR = 512
STEPS = 6
F32 = jnp.float32
MESH = pl.DeviceIdType.MESH
PAD = 8
CH = 32


def join_slabs(left, right):
    head_l, tail_l, tl = left
    head_r, tail_r, tr = right
    divisor = 1.0 - tl[3] * tr[0]
    mid_value = (tail_l - tl[3] * head_r) / divisor
    mid_left = tl[2] / divisor
    mid_right = -tl[3] * tr[1] / divisor
    next_value = head_r - tr[0] * mid_value
    next_left = -tr[0] * mid_left
    next_right = tr[1] - tr[0] * mid_right
    return (
        head_l - tl[1] * next_value,
        tail_r - tr[2] * mid_value,
        (
            tl[0] - tl[1] * next_left,
            -tl[1] * next_right,
            -tr[2] * mid_left,
            tr[3] - tr[2] * mid_right,
        ),
    )


def interface_rows(members, me, n):
    zero = jnp.zeros_like(members[0][0])
    identity = (zero, zero, (zero, zero - 1.0, zero - 1.0, zero))

    def choose(cond, a, b):
        return jax.tree.map(lambda x, y: jnp.where(cond, x, y), a, b)

    prefix = identity
    own = members[0]
    for k in range(n):
        own = choose(k == me, members[k], own)
        prefix = choose(k < me, join_slabs(prefix, members[k]), prefix)
    suffix = identity
    for k in range(n - 1, -1, -1):
        suffix = choose(k > me, join_slabs(members[k], suffix), suffix)
    combined = join_slabs(own, suffix)
    lower = (prefix[1] - prefix[2][3] * combined[0]) / (1.0 - prefix[2][3] * combined[2][0])
    upper = (suffix[0] - suffix[2][0] * (own[1] - own[2][2] * lower)) / (
        1.0 - suffix[2][0] * own[2][3]
    )
    return lower, upper


def kernel(
    n, naz, R, NTL, NZL,
    v, rc, ac, kc, out,
    F, Y, YE, Q, RCF, ACF, HA, PS, PR, RB0, RBE, RBI, TB, MA, MB, PHI, PSI, DP, DM, A0, SPK, CF, LU, ST,
    az_ss, az_rs, ax_ss, ax_rs, r0_ss, r0_rs, re_ss, re_rs, ri_ss, ri_rs, t_ss, t_rs,
):
    me = lax.axis_index("rad")
    az = lax.axis_index("az")
    ax = lax.axis_index("ax")
    left = lax.rem(az + naz - 1, naz)
    right = lax.rem(az + 1, naz)
    other = 1 - ax
    peers = [lax.rem(me + d, n) for d in range(1, n)]
    NI = NTL - 4

    barrier = pltpu.get_barrier_semaphore()
    for p in peers:
        pl.semaphore_signal(barrier, inc=1, device_id={"rad": p}, device_id_type=MESH)
    for p in (left, right):
        pl.semaphore_signal(barrier, inc=1, device_id={"az": p}, device_id_type=MESH)
    pl.semaphore_signal(barrier, inc=1, device_id={"ax": other}, device_id_type=MESH)
    pl.semaphore_wait(barrier, n + 2)

    def az_copy(s, half, side):
        first, to = ((2, left), (NTL, right))[side]
        return pltpu.make_async_remote_copy(
            src_ref=F.at[pl.ds(first, 2), pl.ds(PAD, R), pl.ds(128 * half, 128)],
            dst_ref=HA.at[s, half, 1 - side], send_sem=az_ss.at[s, half, side],
            recv_sem=az_rs.at[s, half, 1 - side], device_id={"az": to}, device_id_type=MESH)

    def ax_copy(s):
        return pltpu.make_async_remote_copy(
            src_ref=PS.at[s], dst_ref=PR.at[s], send_sem=ax_ss.at[s],
            recv_sem=ax_rs.at[s], device_id={"ax": other}, device_id_type=MESH)

    def rad_send(buf, ss, rs, d):
        return pltpu.make_async_remote_copy(
            src_ref=buf.at[me], dst_ref=buf.at[me], send_sem=ss.at[d],
            recv_sem=rs.at[me], device_id={"rad": peers[d]}, device_id_type=MESH)

    def rad_recv(buf, ss, rs, d):
        return pltpu.make_async_remote_copy(
            src_ref=buf.at[me], dst_ref=buf.at[peers[d]], send_sem=ss.at[d],
            recv_sem=rs.at[peers[d]], device_id={"rad": peers[d]}, device_id_type=MESH)

    lane = lax.broadcasted_iota(jnp.int32, (CH, 128), 1)

    def pack(s):
        for c in range(R // CH):
            rows = pl.ds(PAD + c * CH, CH)
            acc = jnp.zeros((CH, 128), F32)
            for j in range(NTL):
                edge = jnp.where(ax == 0, F[j + 2, rows, pl.ds(NZL - 128, 128)],
                                 F[j + 2, rows, pl.ds(0, 128)])
                acc = jnp.where(lane // 2 == j, pltpu.roll(edge, 2 * j + 2 * (1 - ax), 1), acc)
            PS[s, pl.ds(c * CH, CH), :] = acc

    TILES = NZL // 128

    def stage(ref, scale):
        def body(c, carry):
            rows = pl.ds(pl.multiple_of(c * 128, 128), 128)
            for i in range(TILES):
                x = ref[rows, pl.ds(128 * i, 128)].astype(F32)
                ST[i, rows, :] = x if scale is None else x * scale
            return carry

        lax.fori_loop(0, R * NTL // 128, body, 0)

    def split_read(i, j):
        return ST[i, pl.ds(j, R, stride=NTL), :]

    stage(v, None)
    for j in range(NTL):
        for i in range(TILES):
            F[j + 2, pl.ds(PAD, R), pl.ds(128 * i, 128)] = split_read(i, j)
    RB0[me, 0:NTL, :] = v[0:NTL, :]
    RB0[me, NTL : 2 * NTL, :] = v[(R - 1) * NTL : R * NTL, :]
    for half in range(NZL // 128):
        az_copy(0, half, 0).start()
        az_copy(0, half, 1).start()
    for d in range(n - 1):
        rad_send(RB0, r0_ss, r0_rs, d).start()
    pack(0)
    ax_copy(0).start()

    lane1 = lax.broadcasted_iota(jnp.int32, (1, 128), 1)
    ones = jnp.ones((1, 128), F32)

    def march(i, carry):
        phi, p, psi, m = carry
        k = R - 1 - i
        PHI[pl.ds(i, 1), :] = phi
        PSI[pl.ds(k, 1), :] = psi
        DM[pl.ds(k, 1), :] = m
        p = kc[2, pl.ds(i, 1), :] * phi + kc[5, pl.ds(i, 1), :] * p
        m = kc[6, pl.ds(k, 1), :] * psi + kc[7, pl.ds(k, 1), :] * m
        DP[pl.ds(i, 1), :] = p
        return phi + p, p, psi + m, m

    lax.fori_loop(0, R, march, (ones, ones, ones, ones))
    weight = 1.0 / (kc[1] * (DP[...] * PSI[...] + PHI[...] * DM[...]))
    at_i = lax.broadcasted_iota(jnp.int32, (R, R), 0)
    at_j = lax.broadcasted_iota(jnp.int32, (R, R), 1)
    upper_part = jnp.transpose(PSI[...] * weight)[0:R, :]
    lower_part = jnp.transpose(PHI[...] * weight)[0:R, :]
    inverse = jnp.where(at_i <= at_j, PHI[:, 0:R] * upper_part, PSI[:, 0:R] * lower_part)
    high = inverse.astype(jnp.bfloat16)
    MA[:, 0:R] = high
    MA[:, R : 2 * R] = high
    MB[...] = (inverse - high.astype(F32)).astype(jnp.bfloat16)
    SPK[0] = -kc[0, 0:1, :] * jnp.broadcast_to(inverse[:, 0:1], (R, 128))
    SPK[1] = -kc[1, R - 1 : R, :] * jnp.broadcast_to(inverse[:, R - 1 : R], (R, 128))
    A0[...] = 2.0 - 30.0 * (0.25 / 12.0) - 30.0 * kc[4]
    TB[me, 0:1, :] = SPK[0, 0:1, :]
    TB[me, 1:2, :] = SPK[1, 0:1, :]
    TB[me, 2:3, :] = SPK[0, R - 1 : R, :]
    TB[me, 3:4, :] = SPK[1, R - 1 : R, :]
    TB[me, 4:8, :] = jnp.zeros((4, 128), F32)
    for d in range(n - 1):
        rad_send(TB, t_ss, t_rs, d).start()

    for src, dst, scale in ((rc, RCF, -0.5), (ac, ACF, -1.0 / 12.0)):
        stage(src, scale)
        for j in range(NTL):
            for i in range(TILES):
                dst[j, :, pl.ds(128 * i, 128)] = split_read(i, j)

    for d in range(n - 1):
        rad_recv(RB0, r0_ss, r0_rs, d).wait_recv()
    below = jnp.maximum(me - 1, 0)
    above = jnp.minimum(me + 1, n - 1)
    low0 = jnp.where(me > 0, RB0[below, NTL : 2 * NTL, :], 0.0)
    high0 = jnp.where(me < n - 1, RB0[above, 0:NTL, :], 0.0)
    for j in range(NTL):
        F[j + 2, PAD - 1 : PAD, :] = low0[j : j + 1, :]
        F[j + 2, PAD + R : PAD + R + 1, :] = high0[j : j + 1, :]

    for d in range(n - 1):
        rad_recv(TB, t_ss, t_rs, d).wait_recv()
    members = []
    for k in range(n):
        members.append((
            jnp.where(lane1 == 2 * k, 1.0, 0.0),
            jnp.where(lane1 == 2 * k + 1, 1.0, 0.0),
            tuple(TB[k, q : q + 1, :] for q in range(4)),
        ))
    lower_map, upper_map = interface_rows(members, me, n)
    for m in range(2 * n):
        for h, vec in enumerate((lower_map, upper_map)):
            val = jnp.sum(jnp.where(lane1 == m, vec, 0.0), axis=1, keepdims=True)
            CF[h, m // 2, m % 2 : m % 2 + 1, :] = jnp.broadcast_to(val, (1, 128))

    ml = jnp.where(ax == 1, 1.0, 0.0).astype(F32)
    mr = jnp.where(ax == 0, 1.0, 0.0).astype(F32)

    def wide(x):
        return jnp.concatenate([x] * (NZL // 128), axis=1)

    def solve_one(s, j, inner):
        for c in range(R // CH):
            r0 = c * CH
            rows = pl.ds(PAD + r0, CH)
            f = F[j + 2, rows, :]
            lo = F[j + 2, pl.ds(PAD + r0 - 1, CH), :]
            up = F[j + 2, pl.ds(PAD + r0 + 1, CH), :]
            ct = wide(kc[3, pl.ds(r0, CH), :])
            cl = wide(kc[4, pl.ds(r0, CH), :])
            halo = pltpu.roll(PR[s, pl.ds(r0, CH), :], 128 - 2 * j, 1)
            halo1 = pltpu.roll(halo, 127, 1)
            halo2 = pltpu.roll(halo, 126, 1)
            tiles = [f[:, i * 128 : (i + 1) * 128] for i in range(NZL // 128)]
            shifted = {}
            for k in (1, 2):
                down = [pltpu.roll(t, k, 1) for t in tiles]
                edge = ml * (halo1 if k == 1 else halo)
                shifted[-k] = jnp.concatenate([
                    jnp.where(lane < k, edge if i == 0 else down[i - 1], down[i])
                    for i in range(len(tiles))], axis=1)
                rise = [pltpu.roll(t, 128 - k, 1) for t in tiles]
                edge = mr * (halo1 if k == 1 else halo2)
                shifted[k] = jnp.concatenate([
                    jnp.where(lane >= 128 - k,
                              edge if i == len(tiles) - 1 else rise[i + 1], rise[i])
                    for i in range(len(tiles))], axis=1)
            z1d = shifted[1] - shifted[-1]
            z2d = shifted[2] - shifted[-2]
            z1s = shifted[1] + shifted[-1]
            z2s = shifted[2] + shifted[-2]
            a0 = wide(A0[pl.ds(r0, CH), :])
            q = (
                f * a0
                + RCF[j, pl.ds(r0, CH), :] * (up - lo)
                + ACF[j, pl.ds(r0, CH), :] * (8.0 * z1d - z2d)
                + (0.25 / 12.0) * (16.0 * z1s - z2s)
            )
            cols = pl.ds(pl.multiple_of(j * NZL, NZL), NZL)
            if not inner:
                Y[pl.ds(r0, CH), cols] = q
                continue
            m1, m2 = F[j + 1, rows, :], F[j, rows, :]
            p1, p2 = F[j + 3, rows, :], F[j + 4, rows, :]
            q = q + f * (ct * (8.0 * (p1 - m1) - (p2 - m2)))
            q = q + cl * (16.0 * (p1 + m1) - (p2 + m2))
            qh = q.astype(jnp.bfloat16)
            Q[pl.ds(r0, CH), cols] = qh
            Q[pl.ds(R + r0, CH), cols] = (q - qh.astype(F32)).astype(jnp.bfloat16)

    def edge_terms(half, e):
        j = edge_of(e)
        lanes = pl.ds(128 * half, 128)
        cols = pl.ds(pl.multiple_of(j * NZL + 128 * half, 128), 128)
        packed = pl.ds(pl.multiple_of(e * 128, 128), 128)
        for c in range(R // CH):
            r0 = c * CH
            rows = pl.ds(PAD + r0, CH)
            f = F[j + 2, rows, lanes]
            m1, m2 = F[j + 1, rows, lanes], F[j, rows, lanes]
            p1, p2 = F[j + 3, rows, lanes], F[j + 4, rows, lanes]
            q = (
                Y[pl.ds(r0, CH), cols]
                + f * (kc[3, pl.ds(r0, CH), :] * (8.0 * (p1 - m1) - (p2 - m2)))
                + kc[4, pl.ds(r0, CH), :] * (16.0 * (p1 + m1) - (p2 + m2))
            )
            qh = q.astype(jnp.bfloat16)
            Q[pl.ds(r0, CH), packed] = qh
            Q[pl.ds(R + r0, CH), packed] = (q - qh.astype(F32)).astype(jnp.bfloat16)

    def edge_finish(half, e, low, high):
        j = edge_of(e)
        lanes = pl.ds(128 * half, 128)
        for c in range(R // CH):
            rows = pl.ds(PAD + c * CH, CH)
            here = pl.ds(c * CH, CH)
            F[j + 2, rows, lanes] = (
                YE[here, pl.ds(e * 128, 128)] - SPK[0, here, :] * low
                - SPK[1, here, :] * high - F[j + 2, rows, lanes]
            )
        F[j + 2, PAD - 1 : PAD, lanes] = low - F[j + 2, PAD - 1 : PAD, lanes]
        F[j + 2, PAD + R : PAD + R + 1, lanes] = high - F[j + 2, PAD + R : PAD + R + 1, lanes]

    def multiply(start, width):
        cols = pl.ds(start, width)
        y = jnp.dot(MA[...], Q[:, cols], preferred_element_type=F32)
        Y[:, cols] = y + jnp.dot(MB[...], Q[0:R, cols], preferred_element_type=F32)

    def edge_of(e):
        return e + (NTL - 4) * (e // 2)

    def finish(s, j):
        cols = pl.ds(pl.multiple_of(j * NZL, NZL), NZL)
        low = LU[0:1, cols]
        high = LU[1:2, cols]
        for c in range(R // CH):
            rows = pl.ds(PAD + c * CH, CH)
            F[j + 2, rows, :] = (
                Y[pl.ds(c * CH, CH), cols]
                - wide(SPK[0, pl.ds(c * CH, CH), :]) * low
                - wide(SPK[1, pl.ds(c * CH, CH), :]) * high
                - F[j + 2, rows, :]
            )
        F[j + 2, PAD - 1 : PAD, :] = low - F[j + 2, PAD - 1 : PAD, :]
        F[j + 2, PAD + R : PAD + R + 1, :] = high - F[j + 2, PAD + R : PAD + R + 1, :]

    def ends(buf, s, width):
        res = []
        for h in range(2):
            total = None
            for k in range(n):
                coef = jnp.concatenate([CF[h, k]] * (width // 128), axis=1)
                term = coef * buf[(*s, k)]
                total = term if total is None else total + term
            res.append(total[0:1, :] + total[1:2, :])
        return res

    def step(s, carry):
        ax_copy(s).wait_recv()

        def inner(jj, c):
            solve_one(s, jj + 2, True)
            return c

        lax.fori_loop(0, NI, inner, 0)
        multiply(2 * NZL, NI * NZL)
        mid = pl.ds(2 * NZL, NI * NZL)
        RBI[s, me, 0:1, :] = Y[0:1, mid]
        RBI[s, me, 1:2, :] = Y[R - 1 : R, mid]
        for d in range(n - 1):
            rad_send(RBI.at[s], ri_ss.at[s], ri_rs.at[s], d).start()
        def outer(e, c):
            solve_one(s, edge_of(e), False)
            return c

        lax.fori_loop(0, 4, outer, 0)
        for half in range(NZL // 128):
            lanes = pl.ds(128 * half, 128)
            for side in range(2):
                az_copy(s, half, side).wait_recv()
            for i in range(2):
                F[i, pl.ds(PAD, R), lanes] = HA[s, half, 0, i]
                F[NTL + 2 + i, pl.ds(PAD, R), lanes] = HA[s, half, 1, i]
            for e in range(4):
                edge_terms(half, e)
            y = jnp.dot(MA[...], Q[:, 0:512], preferred_element_type=F32)
            y = y + jnp.dot(MB[...], Q[0:R, 0:512], preferred_element_type=F32)
            YE[...] = y
            RBE[s, half, me, 0:1, :] = y[0:1, :]
            RBE[s, half, me, 1:2, :] = y[R - 1 : R, :]
            buf, ss, rs = RBE.at[s, half], re_ss.at[s, half], re_rs.at[s, half]
            for d in range(n - 1):
                rad_send(buf, ss, rs, d).start()
            for side in range(2):
                az_copy(s, half, side).wait_send()
            for d in range(n - 1):
                rad_recv(buf, ss, rs, d).wait_recv()
            low, high = ends(RBE, (s, half), 512)
            for e in range(4):
                edge_finish(half, e, low[:, e * 128 : (e + 1) * 128],
                            high[:, e * 128 : (e + 1) * 128])

            @pl.when(s < STEPS - 1)
            def _():
                az_copy(s + 1, half, 0).start()
                az_copy(s + 1, half, 1).start()

        for d in range(n - 1):
            rad_recv(RBI.at[s], ri_ss.at[s], ri_rs.at[s], d).wait_recv()
        for h, row in enumerate(ends(RBI, (s,), NI * NZL)):
            LU[h : h + 1, mid] = row

        def inner2(jj, c):
            finish(s, jj + 2)
            return c

        lax.fori_loop(0, NI, inner2, 0)

        @pl.when(s < STEPS - 1)
        def _():
            pack(s + 1)
            ax_copy(s + 1).start()

        ax_copy(s).wait_send()
        for d in range(n - 1):
            for half in range(NZL // 128):
                rad_send(RBE.at[s, half], re_ss.at[s, half], re_rs.at[s, half], d).wait_send()
            rad_send(RBI.at[s], ri_ss.at[s], ri_rs.at[s], d).wait_send()
        return carry

    lax.fori_loop(0, STEPS, step, 0)
    for j in range(NTL):
        for i in range(NZL // 128):
            ST[i, pl.ds(j, R, stride=NTL), :] = F[j + 2, pl.ds(PAD, R), pl.ds(128 * i, 128)]

    def unstage(c, carry):
        rows = pl.ds(pl.multiple_of(c * 128, 128), 128)
        for i in range(TILES):
            out[rows, pl.ds(128 * i, 128)] = ST[i, rows, :]
        return carry

    lax.fori_loop(0, R * NTL // 128, unstage, 0)
    for d in range(n - 1):
        rad_send(RB0, r0_ss, r0_rs, d).wait_send()
        rad_send(TB, t_ss, t_rs, d).wait_send()


def local(n, naz, velocity, radial_courant, axial_courant, radial_diffusion):
    R, NTL, NZL = velocity.shape
    position = (lax.axis_index("rad") * R).astype(F32) + jnp.arange(R).astype(F32)
    spacing = 1.0 / (NR + 1)
    radius = 1.0 + (position + 1.0) * spacing
    inward = radial_diffusion * (radius - 0.5 * spacing) / radius
    outward = radial_diffusion * (radius + 0.5 * spacing) / radius
    sink = radial_diffusion * spacing * spacing / (radius * radius)
    grow = 1.0 + sink
    kc = jnp.stack([inward, outward, grow / outward, -(0.25 / 12.0) / radius,
                    (0.25 / 12.0) / (radius * radius), inward / outward,
                    grow / inward, outward / inward])
    kc = jnp.broadcast_to(kc[:, :, None], (8, R, 128))
    flat = lambda a: a.reshape(R * NTL, NZL)
    S = STEPS
    dma = pltpu.SemaphoreType.DMA
    res = pl.pallas_call(
        functools.partial(kernel, n, naz, R, NTL, NZL),
        out_shape=jax.ShapeDtypeStruct((R * NTL, NZL), F32),
        in_specs=[pl.BlockSpec(memory_space=pltpu.VMEM)] * 4,
        out_specs=pl.BlockSpec(memory_space=pltpu.VMEM),
        scratch_shapes=[
            pltpu.VMEM((NTL + 4, R + 2 * PAD, NZL), F32),
            pltpu.VMEM((R, NTL * NZL), F32),
            pltpu.VMEM((R, 512), F32),
            pltpu.VMEM((2 * R, NTL * NZL), jnp.bfloat16),
            pltpu.VMEM((NTL, R, NZL), F32),
            pltpu.VMEM((NTL, R, NZL), F32),
            pltpu.VMEM((S, NZL // 128, 2, 2, R, 128), F32),
            pltpu.VMEM((S, R, 128), F32),
            pltpu.VMEM((S, R, 128), F32),
            pltpu.VMEM((n, 2 * NTL, NZL), F32),
            pltpu.VMEM((S, NZL // 128, n, 2, 512), F32),
            pltpu.VMEM((S, n, 2, (NTL - 4) * NZL), F32),
            pltpu.VMEM((n, 8, 128), F32),
            pltpu.VMEM((R, 2 * R), jnp.bfloat16),
            pltpu.VMEM((R, R), jnp.bfloat16),
            pltpu.VMEM((R, 128), F32),
            pltpu.VMEM((R, 128), F32),
            pltpu.VMEM((R, 128), F32),
            pltpu.VMEM((R, 128), F32),
            pltpu.VMEM((R, 128), F32),
            pltpu.VMEM((2, R, 128), F32),
            pltpu.VMEM((2, n, 2, 128), F32),
            pltpu.VMEM((2, NTL * NZL), F32),
            pltpu.VMEM((NZL // 128, R * NTL, 128), F32),
            dma((S, NZL // 128, 2)), dma((S, NZL // 128, 2)), dma((S,)), dma((S,)),
            dma((n,)), dma((n,)), dma((S, NZL // 128, n)), dma((S, NZL // 128, n)),
            dma((S, n)), dma((S, n)), dma((n,)), dma((n,)),
        ],
        compiler_params=pltpu.CompilerParams(
            collective_id=0, has_side_effects=True, vmem_limit_bytes=48 * 1024 * 1024),
    )(flat(velocity), flat(radial_courant), flat(axial_courant), kc)
    return res.reshape(R, NTL, NZL)


def solution(mesh):
    return jax.shard_map(
        functools.partial(local, mesh.shape["rad"], mesh.shape["az"]),
        mesh=mesh,
        in_specs=(P("rad", "az", "ax"), P("rad", "az", "ax"), P("rad", "az", "ax"), P("rad")),
        out_specs=P("rad", "az", "ax"),
        check_vma=False,
    )
```

profile of v0, /device:TPU:0, one launch (start us, length us, event | category | flops | bytes accessed | tf_op | source)
XLA Modules:
  0.0 123.5 jit_solution(6755201987859003787)
XLA Ops:
  0.0 0.7 divide_bitcast_fusion
  0.7 0.7 divide_bitcast_fusion.1
  1.4 0.2 broadcast_in_dim.2.kc
  1.6 0.0 copy-start
  1.6 1.2 copy-done
  2.8 0.0 copy-start.1
  2.8 1.2 copy-done.1
  4.1 118.1 %shard_map.46 = f32[2048,256]{1,0:T(8,128)S(1)} custom-call(f32[2048,256]{1,0:T(8,128)} %bitcast.19, bf16[2048,256]{1,0:T(8,128)(2,1)S(1)} %bitcast.17, bf16[2048,256]{1,0:T(8,128)(2,1)S(1)} %bitcast.18, f32[8,128,128]{2,1,0:T(8,128)S(1)} %broadcast_in_dim.2.kc), custom_call_target="tpu_custom_call" | custom-call | tf_op jit(solution)/shard_map/pallas_call | solution.py:444
  122.1 1.3 %copy.6 = f32[128,16,256]{2,1,0:T(8,128)} copy(f32[128,16,256]{2,1,0:T(8,128)S(1)} %bitcast.16) | data formatting | bytes 4194304
  (3 shorter events, 0.1 us)
Async XLA Ops:
  1.6 1.2 copy-start
  2.8 1.2 copy-start.1
where the time goes:
time: 124 us; the launch traced here: 123 us
  Pallas kernels  118 us (95%)
  local copies, waits for them, and re-layouts  3.99 us (3%)
  other arithmetic  1.37 us (1%)
    pallas_call x1, Pallas kernels, local(): pl.pallas_call(functools.partial(kernel, n, naz, R, NTL, NZL), out_shape=...  118 us
    unnamed x5, local copies, waits for them, and re-layouts  3.77 us

commit v1 on v0

v1 whole, which is shorter than its diff:
```python
import functools

import jax
import jax.numpy as jnp
from jax import lax
from jax.experimental import pallas as pl
from jax.experimental.pallas import tpu as pltpu
from jax.sharding import PartitionSpec as P

NR = 512
STEPS = 6
F32 = jnp.float32
MESH = pl.DeviceIdType.MESH
PAD = 8
CH = 16


def join_slabs(left, right):
    head_l, tail_l, tl = left
    head_r, tail_r, tr = right
    divisor = 1.0 - tl[3] * tr[0]
    mid_value = (tail_l - tl[3] * head_r) / divisor
    mid_left = tl[2] / divisor
    mid_right = -tl[3] * tr[1] / divisor
    next_value = head_r - tr[0] * mid_value
    next_left = -tr[0] * mid_left
    next_right = tr[1] - tr[0] * mid_right
    return (
        head_l - tl[1] * next_value,
        tail_r - tr[2] * mid_value,
        (
            tl[0] - tl[1] * next_left,
            -tl[1] * next_right,
            -tr[2] * mid_left,
            tr[3] - tr[2] * mid_right,
        ),
    )


def interface_rows(members, me, n):
    zero = jnp.zeros_like(members[0][0])
    identity = (zero, zero, (zero, zero - 1.0, zero - 1.0, zero))

    def choose(cond, a, b):
        return jax.tree.map(lambda x, y: jnp.where(cond, x, y), a, b)

    prefix = identity
    own = members[0]
    for k in range(n):
        own = choose(k == me, members[k], own)
        prefix = choose(k < me, join_slabs(prefix, members[k]), prefix)
    suffix = identity
    for k in range(n - 1, -1, -1):
        suffix = choose(k > me, join_slabs(members[k], suffix), suffix)
    combined = join_slabs(own, suffix)
    lower = (prefix[1] - prefix[2][3] * combined[0]) / (1.0 - prefix[2][3] * combined[2][0])
    upper = (suffix[0] - suffix[2][0] * (own[1] - own[2][2] * lower)) / (
        1.0 - suffix[2][0] * own[2][3]
    )
    return lower, upper


SCALE = 48.0


def kernel(
    n, naz, R, NTL, NZL,
    v, rc, ac, rd, out,
    F, FB, HA, Y, YE, Q, QE, SC, SCE, RCF, ACF, BW, PS, PR, RB0, RBE, RBI, TB, MA, MB, KC,
    PHI, PSI, DP, DM, A0, SPK, CF, LU, ST, STB,
    az_ss, az_rs, ax_ss, ax_rs, r0_ss, r0_rs, re_ss, re_rs, ri_ss, ri_rs, t_ss, t_rs,
    v_s, rb_s, cb_s, cc_s, o_s,
):
    me = lax.axis_index("rad")
    az = lax.axis_index("az")
    ax = lax.axis_index("ax")
    left = lax.rem(az + naz - 1, naz)
    right = lax.rem(az + 1, naz)
    other = 1 - ax
    near, far = 1 - ax, ax
    peers = [lax.rem(me + d, n) for d in range(1, n)]
    GI = (NTL - 4) // 4
    first_of = (2, 2 + 3 * GI, 2 + GI, 2 + 2 * GI)
    edge_first = (0, NTL - 2)
    bf = jnp.bfloat16

    def v_copy(t, j):
        return pltpu.make_async_copy(
            v.at[:, j, pl.ds(128 * t, 128)], F.at[0, t, j, pl.ds(PAD, R), :], v_s.at[t, j])

    def o_copy(t, j):
        return pltpu.make_async_copy(
            F.at[STEPS % 2, t, j, pl.ds(PAD, R), :],
            out.at[:, j, pl.ds(128 * t, 128)], o_s.at[t, j])

    edges = (0, 1, NTL - 2, NTL - 1)
    for j in edges:
        for t in range(2):
            v_copy(t, j).start()
    row_copies = [
        pltpu.make_async_copy(v.at[r], RB0.at[me, pl.ds(q * NTL, NTL), :], rb_s.at[q])
        for q, r in enumerate((0, R - 1))]
    for c in row_copies:
        c.start()
    for j in range(2, NTL - 2):
        for t in range(2):
            v_copy(t, j).start()
    coef_copies = [
        pltpu.make_async_copy(src, STB.at[q], cb_s.at[q]) for q, src in enumerate((rc, ac))]
    for c in coef_copies:
        c.start()

    barrier = pltpu.get_barrier_semaphore()
    for p in peers:
        pl.semaphore_signal(barrier, inc=1, device_id={"rad": p}, device_id_type=MESH)
    for p in (left, right):
        pl.semaphore_signal(barrier, inc=1, device_id={"az": p}, device_id_type=MESH)
    pl.semaphore_signal(barrier, inc=1, device_id={"ax": other}, device_id_type=MESH)
    pl.semaphore_wait(barrier, n + 2)

    def tile_of(p):
        return near if p < 2 else far

    def az_copy(s, p):
        side = p % 2
        return pltpu.make_async_remote_copy(
            src_ref=F.at[lax.rem(s, 2), tile_of(p), pl.ds(edge_first[side], 2), pl.ds(PAD, R), :],
            dst_ref=HA.at[s, p ^ 1], send_sem=az_ss.at[s, p],
            recv_sem=az_rs.at[s, p ^ 1], device_id={"az": (left, right)[side]},
            device_id_type=MESH)

    def ax_copy(s, m):
        return pltpu.make_async_remote_copy(
            src_ref=PS.at[s, m], dst_ref=PR.at[s, m], send_sem=ax_ss.at[s, m],
            recv_sem=ax_rs.at[s, m], device_id={"ax": other}, device_id_type=MESH)

    def rad_send(buf, ss, rs, d):
        return pltpu.make_async_remote_copy(
            src_ref=buf.at[me], dst_ref=buf.at[me], send_sem=ss.at[d],
            recv_sem=rs.at[me], device_id={"rad": peers[d]}, device_id_type=MESH)

    def rad_recv(buf, ss, rs, d):
        return pltpu.make_async_remote_copy(
            src_ref=buf.at[me], dst_ref=buf.at[peers[d]], send_sem=ss.at[d],
            recv_sem=rs.at[peers[d]], device_id={"rad": peers[d]}, device_id_type=MESH)

    for j in edges:
        for t in range(2):
            v_copy(t, j).wait()
    for p in range(4):
        az_copy(0, p).start()
    for c in row_copies:
        c.wait()
    for d in range(n - 1):
        rad_send(RB0, r0_ss, r0_rs, d).start()

    lane = lax.broadcasted_iota(jnp.int32, (CH, 128), 1)

    def members_of(m):
        inner = [first_of[m] + i for i in range(GI)]
        return ([edge_first[m], edge_first[m] + 1] if m < 2 else []) + inner

    def pack(s, m):
        b = lax.rem(s, 2)
        for c in range(R // CH):
            acc = jnp.zeros((CH, 128), F32)
            for i, j in enumerate(members_of(m)):
                edge = F[b, near, j, pl.ds(PAD + c * CH, CH), :]
                acc = jnp.where(lane // 2 == i, pltpu.roll(edge, 2 * i + 2 * (1 - ax), 1), acc)
            PS[s, m, pl.ds(c * CH, CH), :] = acc

    def unpack(s, m):
        for c in range(R // CH):
            rows = pl.ds(c * CH, CH)
            x = PR[s, m, rows, :]
            high = x.astype(bf).astype(F32)
            x = jnp.where(lane < 64, high, pltpu.roll(x - high, 64, 1))
            for i, j in enumerate(members_of(m)):
                FB[j, rows, pl.ds(512, 128)] = jnp.where((lane % 64) // 2 == i, x, 0.0).astype(bf)

    def split_store(j, rows, t, x):
        high = x.astype(bf)
        at = pl.multiple_of(t * 128, 128) if not isinstance(t, int) else t * 128
        FB[j, rows, pl.ds(at, 128)] = high
        FB[j, rows, pl.ds(256 + at, 128)] = (x - high.astype(F32)).astype(bf)

    for j in range(2, NTL - 2):
        for t in range(2):
            v_copy(t, j).wait()

    def first_split(j, carry):
        for t in range(2):
            for c in range(R // CH):
                rows = pl.ds(c * CH, CH)
                split_store(j, rows, t, F[0, t, j, pl.ds(PAD + c * CH, CH), :])
        return carry

    for m in range(4):
        pack(0, m)
        ax_copy(0, m).start()
    lax.fori_loop(0, NTL, first_split, 0)

    row = lax.broadcasted_iota(jnp.int32, (R, 128), 0)
    spacing = 1.0 / (NR + 1)
    radius = 1.0 + ((me * R + row).astype(F32) + 1.0) * spacing
    rdiff = jnp.transpose(jnp.broadcast_to(
        jnp.concatenate([rd[...]] * (128 // R), axis=1), (128, 128)))[0:R, :]
    inward = rdiff * (radius - 0.5 * spacing) / radius
    outward = rdiff * (radius + 0.5 * spacing) / radius
    sink = rdiff * spacing * spacing / (radius * radius)
    grow = 1.0 + sink
    KC[0] = inward
    KC[1] = outward
    KC[2] = grow / outward
    KC[3] = -1.0 / radius
    KC[4] = 1.0 / (radius * radius)
    KC[5] = inward / outward
    KC[6] = grow / inward
    KC[7] = outward / inward
    A0[...] = 66.0 - 30.0 * KC[4]

    lane1 = lax.broadcasted_iota(jnp.int32, (1, 128), 1)
    ones = jnp.ones((1, 128), F32)

    def march(i, carry):
        phi, p, psi, m = carry
        k = R - 1 - i
        PHI[pl.ds(i, 1), :] = phi
        PSI[pl.ds(k, 1), :] = psi
        DM[pl.ds(k, 1), :] = m
        p = KC[2, pl.ds(i, 1), :] * phi + KC[5, pl.ds(i, 1), :] * p
        m = KC[6, pl.ds(k, 1), :] * psi + KC[7, pl.ds(k, 1), :] * m
        DP[pl.ds(i, 1), :] = p
        return phi + p, p, psi + m, m

    lax.fori_loop(0, R, march, (ones, ones, ones, ones))
    weight = 1.0 / (KC[1] * (DP[...] * PSI[...] + PHI[...] * DM[...]))
    at_i = lax.broadcasted_iota(jnp.int32, (R, R), 0)
    at_j = lax.broadcasted_iota(jnp.int32, (R, R), 1)
    upper_part = jnp.transpose(PSI[...] * weight)[0:R, :]
    lower_part = jnp.transpose(PHI[...] * weight)[0:R, :]
    inverse = jnp.where(at_i <= at_j, PHI[:, 0:R] * upper_part, PSI[:, 0:R] * lower_part)
    SPK[0] = -KC[0, 0:1, :] * jnp.broadcast_to(inverse[:, 0:1], (R, 128))
    SPK[1] = -KC[1, R - 1 : R, :] * jnp.broadcast_to(inverse[:, R - 1 : R], (R, 128))
    inverse = inverse * (1.0 / SCALE)
    high = inverse.astype(bf)
    MA[:, 0:R] = high
    MA[:, R : 2 * R] = high
    MB[...] = (inverse - high.astype(F32)).astype(bf)
    TB[me, 0:1, :] = SPK[0, 0:1, :]
    TB[me, 1:2, :] = SPK[1, 0:1, :]
    TB[me, 2:3, :] = SPK[0, R - 1 : R, :]
    TB[me, 3:4, :] = SPK[1, R - 1 : R, :]
    TB[me, 4:8, :] = jnp.zeros((4, 128), F32)
    for d in range(n - 1):
        rad_send(TB, t_ss, t_rs, d).start()

    def band(source, t):
        d = source - (128 * t + lax.broadcasted_iota(jnp.int32, (CH, 128), 1))
        slope = (jnp.where(d == 1, -32.0, 0.0) + jnp.where(d == -1, 32.0, 0.0)
                 + jnp.where(d == 2, 4.0, 0.0) + jnp.where(d == -2, -4.0, 0.0))
        curve = (jnp.where(jnp.abs(d) == 1, 16.0, 0.0) - jnp.where(jnp.abs(d) == 2, 1.0, 0.0))
        return slope.astype(bf), curve.astype(bf)

    here = lax.broadcasted_iota(jnp.int32, (CH, 128), 0)

    def bands(c, carry):
        r0 = pl.multiple_of(c * CH, CH)
        for t in range(2):
            slope, curve = band(here + c * CH, t)
            for q in range(2):
                BW[t, pl.ds(pl.multiple_of(q * 256 + r0, CH), CH), 0:128] = slope
                BW[t, pl.ds(pl.multiple_of(q * 256 + r0, CH), CH), 128:256] = curve
        return carry

    lax.fori_loop(0, 256 // CH, bands, 0)
    for t in range(2):
        slope, curve = band(jnp.where(ax == 0, 256 + here % 2, here % 2 - 2), t)
        for c in range(128 // CH):
            BW[t, pl.ds(512 + c * CH, CH), 0:128] = slope
            BW[t, pl.ds(512 + c * CH, CH), 128:256] = curve

    for q, (dst, scale) in enumerate(((RCF, -0.5 * SCALE), (ACF, None))):
        coef_copies[q].wait()
        moves = []
        for t in range(2):
            def convert(c, carry):
                rows = pl.ds(pl.multiple_of(c * 8, 8), 8)
                x = STB[q, rows, :, pl.ds(128 * t, 128)].astype(F32)
                ST[t, rows] = x if scale is None else x * scale
                return carry

            lax.fori_loop(0, R // 8, convert, 0)
            for j in range(NTL):
                moves.append(pltpu.make_async_copy(ST.at[t, :, j, :], dst.at[t, j], cc_s.at[t, j]))
                moves[-1].start()
        for c in moves:
            c.wait()

    for d in range(n - 1):
        rad_recv(RB0, r0_ss, r0_rs, d).wait_recv()
    below = jnp.maximum(me - 1, 0)
    above = jnp.minimum(me + 1, n - 1)
    low0 = jnp.where(me > 0, RB0[below, NTL : 2 * NTL, :], 0.0)
    high0 = jnp.where(me < n - 1, RB0[above, 0:NTL, :], 0.0)
    for j in range(NTL):
        for t in range(2):
            F[0, t, j, PAD - 1 : PAD, :] = low0[j : j + 1, 128 * t : 128 * t + 128]
            F[0, t, j, PAD + R : PAD + R + 1, :] = high0[j : j + 1, 128 * t : 128 * t + 128]

    for d in range(n - 1):
        rad_recv(TB, t_ss, t_rs, d).wait_recv()
    members = []
    for k in range(n):
        members.append((
            jnp.where(lane1 == 2 * k, 1.0, 0.0),
            jnp.where(lane1 == 2 * k + 1, 1.0, 0.0),
            tuple(TB[k, q : q + 1, :] for q in range(4)),
        ))
    lower_map, upper_map = interface_rows(members, me, n)
    for m in range(2 * n):
        for h, vec in enumerate((lower_map, upper_map)):
            val = jnp.sum(jnp.where(lane1 == m, vec, 0.0), axis=1, keepdims=True)
            CF[h, m // 2, m % 2 : m % 2 + 1, :] = jnp.broadcast_to(val, (1, 128))

    def right_side(b, t, j, r0, near_by, slope, curve):
        rows = pl.ds(PAD + r0, CH)
        at = pl.ds(r0, CH)
        f = F[b, t, j, rows, :]
        lo = F[b, t, j, pl.ds(PAD + r0 - 1, CH), :]
        up = F[b, t, j, pl.ds(PAD + r0 + 1, CH), :]
        m2, m1, p1, p2 = near_by
        dt = 8.0 * (p1 - m1) - (p2 - m2)
        lt = 16.0 * (p1 + m1) - (p2 + m2)
        return (
            f * (A0[at, :] + KC[3, at, :] * dt) + KC[4, at, :] * lt
            + RCF[t, j, at, :] * (up - lo) + (ACF[t, j, at, :] * slope + curve)
        )

    def solve(q):
        return (jnp.dot(MA[...], q[...], preferred_element_type=F32)
                + jnp.dot(MB[...], q[0:R, :], preferred_element_type=F32))

    def put_q(q, r0, cols, x):
        high = x.astype(bf)
        q[pl.ds(r0, CH), cols] = high
        q[pl.ds(R + r0, CH), cols] = (x - high.astype(F32)).astype(bf)

    def axial_edges(side):
        lhs = FB[pl.ds(edge_first[side], 2)].reshape(2 * R, 640)
        for t in range(2):
            SCE[side, t] = jnp.dot(lhs, BW[t], preferred_element_type=F32)

    def edge_solve(s, p):
        side = p % 2
        b = lax.rem(s, 2)
        t = tile_of(p)

        def layer(j, r0):
            if j < 0:
                return HA[s, p, 2 + j, pl.ds(r0, CH), :]
            if j >= NTL:
                return HA[s, p, j - NTL, pl.ds(r0, CH), :]
            return F[b, t, j, pl.ds(PAD + r0, CH), :]

        az_copy(s, p ^ 1).wait_recv()
        for i in range(2):
            j = edge_first[side] + i
            for c in range(R // CH):
                r0 = c * CH
                at = pl.ds(i * R + r0, CH)
                x = right_side(
                    b, t, j, r0, [layer(j + o, r0) for o in (-2, -1, 1, 2)],
                    SCE[side, t, at, 0:128], SCE[side, t, at, 128:256])
                put_q(QE, r0, pl.ds(i * 128, 128), x)
        y = solve(QE)
        YE[p] = y
        RBE[s, p, me, 0:1, :] = y[0:1, :]
        RBE[s, p, me, 1:2, :] = y[R - 1 : R, :]
        for d in range(n - 1):
            rad_send(RBE.at[s, p], re_ss.at[s, p], re_rs.at[s, p], d).start()

    def ends(buf, idx, width):
        res = []
        for h in range(2):
            total = None
            for k in range(n):
                coef = jnp.concatenate([CF[h, k]] * (width // 128), axis=1)
                term = coef * buf[(*idx, k)]
                total = term if total is None else total + term
            res.append(total[0:1, :] + total[1:2, :])
        return res

    def advance(b, t, j, y_of, low, high):
        for c in range(R // CH):
            here = pl.ds(c * CH, CH)
            rows = pl.ds(PAD + c * CH, CH)
            x = (y_of(here) - SPK[0, here, :] * low - SPK[1, here, :] * high - F[b, t, j, rows, :])
            F[1 - b, t, j, rows, :] = x
            split_store(j, here, t, x)
        F[1 - b, t, j, PAD - 1 : PAD, :] = low - F[b, t, j, PAD - 1 : PAD, :]
        F[1 - b, t, j, PAD + R : PAD + R + 1, :] = high - F[b, t, j, PAD + R : PAD + R + 1, :]

    def edge_finish(s, p):
        b = lax.rem(s, 2)
        t = tile_of(p)
        buf, ss, rs = RBE.at[s, p], re_ss.at[s, p], re_rs.at[s, p]
        az_copy(s, p).wait_send()
        for d in range(n - 1):
            rad_send(buf, ss, rs, d).wait_send()
        for d in range(n - 1):
            rad_recv(buf, ss, rs, d).wait_recv()
        low, high = ends(RBE, (s, p), 256)
        for i in range(2):
            cols = slice(i * 128, i * 128 + 128)
            advance(b, t, edge_first[p % 2] + i,
                    lambda here: YE[p, here, cols], low[:, cols], high[:, cols])

        @pl.when(s < STEPS - 1)
        def _():
            az_copy(s + 1, p).start()

        if p >= 2:
            @pl.when(s == STEPS - 1)
            def _():
                for i in range(2):
                    for tt in range(2):
                        o_copy(tt, edge_first[p % 2] + i).start()

    def inner_solve(s, k):
        b = lax.rem(s, 2)
        lhs = FB[pl.ds(first_of[k], GI)].reshape(GI * R, 640)
        for t in range(2):
            SC[t] = jnp.dot(lhs, BW[t], preferred_element_type=F32)

        def rhs(i):
            j = first_of[k] + i
            for t in range(2):
                for c in range(R // CH):
                    r0 = c * CH
                    at = pl.ds(pl.multiple_of(i * R + r0, CH), CH)
                    x = right_side(
                        b, t, j, r0,
                        [F[b, t, j + o, pl.ds(PAD + r0, CH), :] for o in (-2, -1, 1, 2)],
                        SC[t, at, 0:128], SC[t, at, 128:256])
                    put_q(Q.at[i], r0, pl.ds(t * 128, 128), x)

        def close(i):
            y = solve(Q.at[i])
            Y[k, i] = y
            cols = pl.ds(pl.multiple_of(i * NZL, NZL), NZL)
            RBI[s, k, me, 0:1, cols] = y[0:1, :]
            RBI[s, k, me, 1:2, cols] = y[R - 1 : R, :]

        rhs(0)

        def body(i, c):
            close(i - 1)
            rhs(i)
            return c

        lax.fori_loop(1, GI, body, 0)
        close(GI - 1)
        for d in range(n - 1):
            rad_send(RBI.at[s, k], ri_ss.at[s, k], ri_rs.at[s, k], d).start()

    def inner_finish(s, k):
        b = lax.rem(s, 2)
        buf, ss, rs = RBI.at[s, k], ri_ss.at[s, k], ri_rs.at[s, k]
        for d in range(n - 1):
            rad_send(buf, ss, rs, d).wait_send()
        for d in range(n - 1):
            rad_recv(buf, ss, rs, d).wait_recv()
        for h, line in enumerate(ends(RBI, (s, k), GI * NZL)):
            LU[h : h + 1, :] = line

        def body(i, c):
            for t in range(2):
                cols = pl.ds(pl.multiple_of(i * NZL + t * 128, 128), 128)
                advance(b, t, first_of[k] + i,
                        lambda here: Y[k, i, here, pl.ds(t * 128, 128)],
                        LU[0:1, cols], LU[1:2, cols])
            return c

        lax.fori_loop(0, GI, body, 0)

        @pl.when(s < STEPS - 1)
        def _():
            pack(s + 1, k)
            ax_copy(s + 1, k).start()

        @pl.when(s == STEPS - 1)
        def _():
            for i in range(GI):
                for t in range(2):
                    o_copy(t, first_of[k] + i).start()

    def step(s, carry):
        for k in range(4):
            ax_copy(s, k).wait_recv()
            unpack(s, k)
            if k < 2:
                axial_edges(k)
            edge_solve(s, k)
            if k < 2:
                @pl.when(s > 0)
                def _():
                    inner_finish(s - 1, k + 2)
            else:
                inner_finish(s, k - 2)
            if k == 0:
                @pl.when(s > 0)
                def _():
                    edge_finish(s - 1, 3)
            else:
                edge_finish(s, k - 1)
            inner_solve(s, k)
            ax_copy(s, k).wait_send()
        return carry

    lax.fori_loop(0, STEPS, step, 0)
    inner_finish(STEPS - 1, 2)
    edge_finish(STEPS - 1, 3)
    inner_finish(STEPS - 1, 3)
    for j in range(NTL):
        for t in range(2):
            o_copy(t, j).wait()
    for d in range(n - 1):
        rad_send(RB0, r0_ss, r0_rs, d).wait_send()
        rad_send(TB, t_ss, t_rs, d).wait_send()


def local(n, naz, velocity, radial_courant, axial_courant, radial_diffusion):
    R, NTL, NZL = velocity.shape
    S = STEPS
    GI = (NTL - 4) // 4
    dma = pltpu.SemaphoreType.DMA
    bf = jnp.bfloat16
    hbm = pl.BlockSpec(memory_space=pl.ANY)
    return pl.pallas_call(
        functools.partial(kernel, n, naz, R, NTL, NZL),
        out_shape=jax.ShapeDtypeStruct((R, NTL, NZL), F32),
        in_specs=[hbm, hbm, hbm, pl.BlockSpec(memory_space=pltpu.VMEM)],
        out_specs=hbm,
        scratch_shapes=[
            pltpu.VMEM((2, 2, NTL, R + 2 * PAD, 128), F32),
            pltpu.VMEM((NTL, R, 640), bf),
            pltpu.VMEM((S, 4, 2, R, 128), F32),
            pltpu.VMEM((4, GI, R, NZL), F32),
            pltpu.VMEM((4, R, 256), F32),
            pltpu.VMEM((GI, 2 * R, NZL), bf),
            pltpu.VMEM((2 * R, 256), bf),
            pltpu.VMEM((2, GI * R, 256), F32),
            pltpu.VMEM((2, 2, 2 * R, 256), F32),
            pltpu.VMEM((2, NTL, R, 128), F32),
            pltpu.VMEM((2, NTL, R, 128), F32),
            pltpu.VMEM((2, 640, 256), bf),
            pltpu.VMEM((S, 4, R, 128), F32),
            pltpu.VMEM((S, 4, R, 128), F32),
            pltpu.VMEM((n, 2 * NTL, NZL), F32),
            pltpu.VMEM((S, 4, n, 2, 256), F32),
            pltpu.VMEM((S, 4, n, 2, GI * NZL), F32),
            pltpu.VMEM((n, 8, 128), F32),
            pltpu.VMEM((R, 2 * R), bf),
            pltpu.VMEM((R, R), bf),
            pltpu.VMEM((8, R, 128), F32),
            pltpu.VMEM((R, 128), F32),
            pltpu.VMEM((R, 128), F32),
            pltpu.VMEM((R, 128), F32),
            pltpu.VMEM((R, 128), F32),
            pltpu.VMEM((R, 128), F32),
            pltpu.VMEM((2, R, 128), F32),
            pltpu.VMEM((2, n, 2, 128), F32),
            pltpu.VMEM((2, GI * NZL), F32),
            pltpu.VMEM((2, R, NTL, 128), F32),
            pltpu.VMEM((2, R, NTL, NZL), bf),
            dma((S, 4)), dma((S, 4)), dma((S, 4)), dma((S, 4)),
            dma((n,)), dma((n,)), dma((S, 4, n)), dma((S, 4, n)),
            dma((S, 4, n)), dma((S, 4, n)), dma((n,)), dma((n,)),
            dma((2, NTL)), dma((2,)), dma((2,)), dma((2, NTL)), dma((2, NTL)),
        ],
        compiler_params=pltpu.CompilerParams(
            collective_id=0, has_side_effects=True, vmem_limit_bytes=58 * 1024 * 1024),
    )(velocity, radial_courant, axial_courant, radial_diffusion.reshape(1, R))


def solution(mesh):
    return jax.shard_map(
        functools.partial(local, mesh.shape["rad"], mesh.shape["az"]),
        mesh=mesh,
        in_specs=(P("rad", "az", "ax"), P("rad", "az", "ax"), P("rad", "az", "ax"), P("rad")),
        out_specs=P("rad", "az", "ax"),
        check_vma=False,
    )
```

time: 124 us -> 103 us (0.83)
  Pallas kernels: 118 us -> 100 us
  other arithmetic: 1.37 us -> 0 us
    pallas_call x1, Pallas kernels: 118 us -> 100 us  [local(): pl.pallas_call(functools.partial(kernel, n, naz, R, NTL, NZL), out_shape=...]
    another operation x3 -> x0, other arithmetic: 1.36 us -> none  [local(): jnp.stack([inward, outward, grow / outward, -(0.25 / 12.0) / radius, 0.25...]
    unnamed x5 -> x1, local copies, waits for them, and re-layouts: 3.77 us -> 3.08 us
where the time goes in v1:
time: 103 us
  Pallas kernels  100 us (97%)
  local copies, waits for them, and re-layouts  3.08 us (3%)
    pallas_call x1, Pallas kernels, local(): pl.pallas_call(functools.partial(kernel, n, naz, R, NTL, NZL), out_shape=...  100 us
    unnamed x1, local copies, waits for them, and re-layouts  3.08 us

profile of v1, /device:TPU:0, one launch (start us, length us, event | category | flops | bytes accessed | tf_op | source)
XLA Modules:
  0.0 103.2 jit_solution(2947306879705309296)
XLA Ops:
  0.0 100.1 %shard_map.46 = f32[128,16,256]{2,1,0:T(8,128)} custom-call(f32[128,16,256]{2,1,0:T(8,128)} %v.1, bf16[128,16,256]{2,1,0:T(8,128)(2,1)} %rc.1, bf16[128,16,256]{2,1,0:T(8,128)(2,1)} %ac.1, f32[1,128]{1,0:T(1,128)} %bitcast.1), custom_call_target="tpu_custom_call" | custom-call | tf_op jit(solution)/shard_map/pallas_call | solution.py:540
  100.1 3.1 %copy.6 = f32[128,16,256]{2,1,0:T(8,128)} copy(f32[128,16,256]{2,1,0:T(8,128)} %shard_map.46) | data formatting | bytes 4194304

commit v2 on v1

--- a/solution.py
+++ b/solution.py
@@ -66,9 +66,9 @@
 def kernel(
     n, naz, R, NTL, NZL,
     v, rc, ac, rd, out,
-    F, FB, HA, Y, YE, Q, QE, SC, SCE, RCF, ACF, BW, PS, PR, RB0, RBE, RBI, TB, MA, MB, KC,
+    F, FB, HA, HX, LS, LR, Y, YE, Q, QE, SC, SCE, RCF, ACF, BW, PS, PR, RB0, RBE, RBI, TB, MA, MB, KC,
     PHI, PSI, DP, DM, A0, SPK, CF, LU, ST, STB,
-    az_ss, az_rs, ax_ss, ax_rs, r0_ss, r0_rs, re_ss, re_rs, ri_ss, ri_rs, t_ss, t_rs,
+    a0_ss, a0_rs, az_ss, az_rs, lh_ss, lh_rs, ax_ss, ax_rs, r0_ss, r0_rs, re_ss, re_rs, ri_ss, ri_rs, t_ss, t_rs,
     v_s, rb_s, cb_s, cc_s, o_s,
 ):
     me = lax.axis_index("rad")
@@ -91,7 +91,7 @@
     def o_copy(t, j):
         return pltpu.make_async_copy(
             F.at[STEPS % 2, t, j, pl.ds(PAD, R), :],
-            out.at[:, j, pl.ds(128 * t, 128)], o_s.at[t, j])
+            out.at[:, j, pl.ds(pl.multiple_of(128 * t, 128), 128)], o_s.at[t, j])
 
     edges = (0, 1, NTL - 2, NTL - 1)
     for j in edges:
@@ -121,12 +121,24 @@
     def tile_of(p):
         return near if p < 2 else far
 
-    def az_copy(s, p):
+    def az_first(p):
         side = p % 2
         return pltpu.make_async_remote_copy(
-            src_ref=F.at[lax.rem(s, 2), tile_of(p), pl.ds(edge_first[side], 2), pl.ds(PAD, R), :],
-            dst_ref=HA.at[s, p ^ 1], send_sem=az_ss.at[s, p],
-            recv_sem=az_rs.at[s, p ^ 1], device_id={"az": (left, right)[side]},
+            src_ref=F.at[0, tile_of(p), pl.ds(edge_first[side], 2), pl.ds(PAD, R), :],
+            dst_ref=HX.at[p ^ 1], send_sem=a0_ss.at[p],
+            recv_sem=a0_rs.at[p ^ 1], device_id={"az": (left, right)[side]},
+            device_id_type=MESH)
+
+    def az_copy(s, p):
+        return pltpu.make_async_remote_copy(
+            src_ref=YE.at[s - 1, p], dst_ref=HA.at[s - 1, p ^ 1], send_sem=az_ss.at[s - 1, p],
+            recv_sem=az_rs.at[s - 1, p ^ 1], device_id={"az": (left, right)[p % 2]},
+            device_id_type=MESH)
+
+    def lh_copy(s, p):
+        return pltpu.make_async_remote_copy(
+            src_ref=LS.at[s - 1, p], dst_ref=LR.at[s - 1, p ^ 1], send_sem=lh_ss.at[s - 1, p],
+            recv_sem=lh_rs.at[s - 1, p ^ 1], device_id={"az": (left, right)[p % 2]},
             device_id_type=MESH)
 
     def ax_copy(s, m):
@@ -147,8 +159,8 @@
     for j in edges:
         for t in range(2):
             v_copy(t, j).wait()
-    for p in range(4):
-        az_copy(0, p).start()
+    for p in range(2):
+        az_first(p).start()
     for c in row_copies:
         c.wait()
     for d in range(n - 1):
@@ -199,6 +211,8 @@
         pack(0, m)
         ax_copy(0, m).start()
     lax.fori_loop(0, NTL, first_split, 0)
+    for p in range(2, 4):
+        az_first(p).start()
 
     row = lax.broadcasted_iota(jnp.int32, (R, 128), 0)
     spacing = 1.0 / (NR + 1)
@@ -358,12 +372,31 @@
 
         def layer(j, r0):
             if j < 0:
-                return HA[s, p, 2 + j, pl.ds(r0, CH), :]
+                return HX[p, 2 + j, pl.ds(r0, CH), :]
             if j >= NTL:
-                return HA[s, p, j - NTL, pl.ds(r0, CH), :]
+                return HX[p, j - NTL, pl.ds(r0, CH), :]
             return F[b, t, j, pl.ds(PAD + r0, CH), :]
 
-        az_copy(s, p ^ 1).wait_recv()
+        @pl.when(s == 0)
+        def _():
+            az_first(p ^ 1).wait_recv()
+            az_first(p).wait_send()
+
+        @pl.when(s > 0)
+        def _():
+            for copy in (az_copy, lh_copy):
+                copy(s, p ^ 1).wait_recv()
+                copy(s, p).wait_send()
+            for i in range(2):
+                cols = slice(i * 128, i * 128 + 128)
+                low = LR[s - 1, p, 0:1, cols]
+                high = LR[s - 1, p, 1:2, cols]
+                for c in range(R // CH):
+                    here = pl.ds(c * CH, CH)
+                    HX[p, i, here, :] = (
+                        HA[s - 1, p, here, cols] - SPK[0, here, :] * low
+                        - SPK[1, here, :] * high - HX[p, i, here, :])
+
         for i in range(2):
             j = edge_first[side] + i
             for c in range(R // CH):
@@ -374,11 +407,15 @@
                     SCE[side, t, at, 0:128], SCE[side, t, at, 128:256])
                 put_q(QE, r0, pl.ds(i * 128, 128), x)
         y = solve(QE)
-        YE[p] = y
+        YE[s, p] = y
         RBE[s, p, me, 0:1, :] = y[0:1, :]
         RBE[s, p, me, 1:2, :] = y[R - 1 : R, :]
         for d in range(n - 1):
             rad_send(RBE.at[s, p], re_ss.at[s, p], re_rs.at[s, p], d).start()
+
+        @pl.when(s < STEPS - 1)
+        def _():
+            az_copy(s + 1, p).start()
 
     def ends(buf, idx, width):
         res = []
@@ -405,27 +442,27 @@
         b = lax.rem(s, 2)
         t = tile_of(p)
         buf, ss, rs = RBE.at[s, p], re_ss.at[s, p], re_rs.at[s, p]
-        az_copy(s, p).wait_send()
         for d in range(n - 1):
             rad_send(buf, ss, rs, d).wait_send()
         for d in range(n - 1):
             rad_recv(buf, ss, rs, d).wait_recv()
         low, high = ends(RBE, (s, p), 256)
+
+        @pl.when(s < STEPS - 1)
+        def _():
+            LS[s, p, 0:1, :] = low
+            LS[s, p, 1:2, :] = high
+            lh_copy(s + 1, p).start()
+
         for i in range(2):
             cols = slice(i * 128, i * 128 + 128)
             advance(b, t, edge_first[p % 2] + i,
-                    lambda here: YE[p, here, cols], low[:, cols], high[:, cols])
-
-        @pl.when(s < STEPS - 1)
+                    lambda here: YE[s, p, here, cols], low[:, cols], high[:, cols])
+
+        @pl.when(s == STEPS - 1)
         def _():
-            az_copy(s + 1, p).start()
-
-        if p >= 2:
-            @pl.when(s == STEPS - 1)
-            def _():
-                for i in range(2):
-                    for tt in range(2):
-                        o_copy(tt, edge_first[p % 2] + i).start()
+            for i in range(2):
+                o_copy(t, edge_first[p % 2] + i).start()
 
     def inner_solve(s, k):
         b = lax.rem(s, 2)
@@ -499,29 +536,24 @@
         for k in range(4):
             ax_copy(s, k).wait_recv()
             unpack(s, k)
+            inner_solve(s, k)
             if k < 2:
                 axial_edges(k)
             edge_solve(s, k)
-            if k < 2:
-                @pl.when(s > 0)
-                def _():
-                    inner_finish(s - 1, k + 2)
-            else:
-                inner_finish(s, k - 2)
             if k == 0:
                 @pl.when(s > 0)
                 def _():
                     edge_finish(s - 1, 3)
+                    inner_finish(s - 1, 3)
             else:
                 edge_finish(s, k - 1)
-            inner_solve(s, k)
+                inner_finish(s, k - 1)
             ax_copy(s, k).wait_send()
         return carry
 
     lax.fori_loop(0, STEPS, step, 0)
-    inner_finish(STEPS - 1, 2)
+    inner_finish(STEPS - 1, 3)
     edge_finish(STEPS - 1, 3)
-    inner_finish(STEPS - 1, 3)
     for j in range(NTL):
         for t in range(2):
             o_copy(t, j).wait()
@@ -545,9 +577,12 @@
         scratch_shapes=[
             pltpu.VMEM((2, 2, NTL, R + 2 * PAD, 128), F32),
             pltpu.VMEM((NTL, R, 640), bf),
-            pltpu.VMEM((S, 4, 2, R, 128), F32),
+            pltpu.VMEM((S - 1, 4, R, 256), F32),
+            pltpu.VMEM((4, 2, R, 128), F32),
+            pltpu.VMEM((S - 1, 4, 2, 256), F32),
+            pltpu.VMEM((S - 1, 4, 2, 256), F32),
             pltpu.VMEM((4, GI, R, NZL), F32),
-            pltpu.VMEM((4, R, 256), F32),
+            pltpu.VMEM((S, 4, R, 256), F32),
             pltpu.VMEM((GI, 2 * R, NZL), bf),
             pltpu.VMEM((2 * R, 256), bf),
             pltpu.VMEM((2, GI * R, 256), F32),
@@ -574,7 +609,8 @@
             pltpu.VMEM((2, GI * NZL), F32),
             pltpu.VMEM((2, R, NTL, 128), F32),
             pltpu.VMEM((2, R, NTL, NZL), bf),
-            dma((S, 4)), dma((S, 4)), dma((S, 4)), dma((S, 4)),
+            dma((4,)), dma((4,)), dma((S - 1, 4)), dma((S - 1, 4)), dma((S - 1, 4)), dma((S - 1, 4)),
+            dma((S, 4)), dma((S, 4)),
             dma((n,)), dma((n,)), dma((S, 4, n)), dma((S, 4, n)),
             dma((S, 4, n)), dma((S, 4, n)), dma((n,)), dma((n,)),
             dma((2, NTL)), dma((2,)), dma((2,)), dma((2, NTL)), dma((2, NTL)),

time: 103 us -> 94.5 us (0.917)
  Pallas kernels: 100 us -> 91.3 us
    pallas_call x1, Pallas kernels: 100 us -> 91.3 us  [local(): pl.pallas_call(functools.partial(kernel, n, naz, R, NTL, NZL), out_shape=...]
where the time goes in v2:
time: 94.5 us; the launch traced here: 94.3 us
  Pallas kernels  91.3 us (97%)
  local copies, waits for them, and re-layouts  3.08 us (3%)
    pallas_call x1, Pallas kernels, local(): pl.pallas_call(functools.partial(kernel, n, naz, R, NTL, NZL), out_shape=...  91.3 us
    unnamed x1, local copies, waits for them, and re-layouts  3.08 us

profile of v2, /device:TPU:0, one launch (start us, length us, event | category | flops | bytes accessed | tf_op | source)
XLA Modules:
  0.0 94.3 jit_solution(8003637960173216411)
XLA Ops:
  0.0 91.3 %shard_map.46 = f32[128,16,256]{2,1,0:T(8,128)} custom-call(f32[128,16,256]{2,1,0:T(8,128)} %v.1, bf16[128,16,256]{2,1,0:T(8,128)(2,1)} %rc.1, bf16[128,16,256]{2,1,0:T(8,128)(2,1)} %ac.1, f32[1,128]{1,0:T(1,128)} %bitcast.1), custom_call_target="tpu_custom_call" | custom-call | tf_op jit(solution)/shard_map/pallas_call | solution.py:572
  91.3 3.1 %copy.6 = f32[128,16,256]{2,1,0:T(8,128)} copy(f32[128,16,256]{2,1,0:T(8,128)} %shard_map.46) | data formatting | bytes 4194304

commit v3 on v2

--- a/solution.py
+++ b/solution.py
@@ -66,10 +66,10 @@
 def kernel(
     n, naz, R, NTL, NZL,
     v, rc, ac, rd, out,
-    F, FB, HA, HX, LS, LR, Y, YE, Q, QE, SC, SCE, RCF, ACF, BW, PS, PR, RB0, RBE, RBI, TB, MA, MB, KC,
-    PHI, PSI, DP, DM, A0, SPK, CF, LU, ST, STB,
+    F, FB, HA, LS, LR, Y, YE, Q, QE, SC, SCE, RCF, ACF, BW, PS, PR, RB0, RBE, RBI, TB, MA, MB, KC,
+    PHI, PSI, DP, DM, A0, SPK, CF, STB,
     a0_ss, a0_rs, az_ss, az_rs, lh_ss, lh_rs, ax_ss, ax_rs, r0_ss, r0_rs, re_ss, re_rs, ri_ss, ri_rs, t_ss, t_rs,
-    v_s, rb_s, cb_s, cc_s, o_s,
+    v_s, rb_s, cb_s, o_s,
 ):
     me = lax.axis_index("rad")
     az = lax.axis_index("az")
@@ -80,17 +80,28 @@
     near, far = 1 - ax, ax
     peers = [lax.rem(me + d, n) for d in range(1, n)]
     GI = (NTL - 4) // 4
-    first_of = (2, 2 + 3 * GI, 2 + GI, 2 + 2 * GI)
-    edge_first = (0, NTL - 2)
+    parity = lax.rem(az, 2)
+
+    def group(k, q):
+        lowest = (2, 2 + 3 * GI, 2 + GI, 2 + 2 * GI)
+        return lowest[k] if q == 0 else lowest[k ^ 1]
+
+    def edge(p, q):
+        return (NTL - 2) * ((p % 2) ^ q)
+
+    first_of = [group(k, 0) + parity * (group(k, 1) - group(k, 0)) for k in range(4)]
+    edge_first = [edge(p, 0) + parity * (edge(p, 1) - edge(p, 0)) for p in range(2)]
+    side_of = [p + parity * (1 - 2 * p) for p in range(2)]
+    beside = [lax.rem(az + naz - 1 + 2 * side_of[p], naz) for p in range(2)]
     bf = jnp.bfloat16
 
     def v_copy(t, j):
         return pltpu.make_async_copy(
-            v.at[:, j, pl.ds(128 * t, 128)], F.at[0, t, j, pl.ds(PAD, R), :], v_s.at[t, j])
+            v.at[:, j, pl.ds(128 * t, 128)], F.at[0, t, j + 2, pl.ds(PAD, R), :], v_s.at[t, j])
 
     def o_copy(t, j):
         return pltpu.make_async_copy(
-            F.at[STEPS % 2, t, j, pl.ds(PAD, R), :],
+            F.at[STEPS % 2, t, j + 2, pl.ds(PAD, R), :],
             out.at[:, j, pl.ds(pl.multiple_of(128 * t, 128), 128)], o_s.at[t, j])
 
     edges = (0, 1, NTL - 2, NTL - 1)
@@ -116,104 +127,6 @@
     for p in (left, right):
         pl.semaphore_signal(barrier, inc=1, device_id={"az": p}, device_id_type=MESH)
     pl.semaphore_signal(barrier, inc=1, device_id={"ax": other}, device_id_type=MESH)
-    pl.semaphore_wait(barrier, n + 2)
-
-    def tile_of(p):
-        return near if p < 2 else far
-
-    def az_first(p):
-        side = p % 2
-        return pltpu.make_async_remote_copy(
-            src_ref=F.at[0, tile_of(p), pl.ds(edge_first[side], 2), pl.ds(PAD, R), :],
-            dst_ref=HX.at[p ^ 1], send_sem=a0_ss.at[p],
-            recv_sem=a0_rs.at[p ^ 1], device_id={"az": (left, right)[side]},
-            device_id_type=MESH)
-
-    def az_copy(s, p):
-        return pltpu.make_async_remote_copy(
-            src_ref=YE.at[s - 1, p], dst_ref=HA.at[s - 1, p ^ 1], send_sem=az_ss.at[s - 1, p],
-            recv_sem=az_rs.at[s - 1, p ^ 1], device_id={"az": (left, right)[p % 2]},
-            device_id_type=MESH)
-
-    def lh_copy(s, p):
-        return pltpu.make_async_remote_copy(
-            src_ref=LS.at[s - 1, p], dst_ref=LR.at[s - 1, p ^ 1], send_sem=lh_ss.at[s - 1, p],
-            recv_sem=lh_rs.at[s - 1, p ^ 1], device_id={"az": (left, right)[p % 2]},
-            device_id_type=MESH)
-
-    def ax_copy(s, m):
-        return pltpu.make_async_remote_copy(
-            src_ref=PS.at[s, m], dst_ref=PR.at[s, m], send_sem=ax_ss.at[s, m],
-            recv_sem=ax_rs.at[s, m], device_id={"ax": other}, device_id_type=MESH)
-
-    def rad_send(buf, ss, rs, d):
-        return pltpu.make_async_remote_copy(
-            src_ref=buf.at[me], dst_ref=buf.at[me], send_sem=ss.at[d],
-            recv_sem=rs.at[me], device_id={"rad": peers[d]}, device_id_type=MESH)
-
-    def rad_recv(buf, ss, rs, d):
-        return pltpu.make_async_remote_copy(
-            src_ref=buf.at[me], dst_ref=buf.at[peers[d]], send_sem=ss.at[d],
-            recv_sem=rs.at[peers[d]], device_id={"rad": peers[d]}, device_id_type=MESH)
-
-    for j in edges:
-        for t in range(2):
-            v_copy(t, j).wait()
-    for p in range(2):
-        az_first(p).start()
-    for c in row_copies:
-        c.wait()
-    for d in range(n - 1):
-        rad_send(RB0, r0_ss, r0_rs, d).start()
-
-    lane = lax.broadcasted_iota(jnp.int32, (CH, 128), 1)
-
-    def members_of(m):
-        inner = [first_of[m] + i for i in range(GI)]
-        return ([edge_first[m], edge_first[m] + 1] if m < 2 else []) + inner
-
-    def pack(s, m):
-        b = lax.rem(s, 2)
-        for c in range(R // CH):
-            acc = jnp.zeros((CH, 128), F32)
-            for i, j in enumerate(members_of(m)):
-                edge = F[b, near, j, pl.ds(PAD + c * CH, CH), :]
-                acc = jnp.where(lane // 2 == i, pltpu.roll(edge, 2 * i + 2 * (1 - ax), 1), acc)
-            PS[s, m, pl.ds(c * CH, CH), :] = acc
-
-    def unpack(s, m):
-        for c in range(R // CH):
-            rows = pl.ds(c * CH, CH)
-            x = PR[s, m, rows, :]
-            high = x.astype(bf).astype(F32)
-            x = jnp.where(lane < 64, high, pltpu.roll(x - high, 64, 1))
-            for i, j in enumerate(members_of(m)):
-                FB[j, rows, pl.ds(512, 128)] = jnp.where((lane % 64) // 2 == i, x, 0.0).astype(bf)
-
-    def split_store(j, rows, t, x):
-        high = x.astype(bf)
-        at = pl.multiple_of(t * 128, 128) if not isinstance(t, int) else t * 128
-        FB[j, rows, pl.ds(at, 128)] = high
-        FB[j, rows, pl.ds(256 + at, 128)] = (x - high.astype(F32)).astype(bf)
-
-    for j in range(2, NTL - 2):
-        for t in range(2):
-            v_copy(t, j).wait()
-
-    def first_split(j, carry):
-        for t in range(2):
-            for c in range(R // CH):
-                rows = pl.ds(c * CH, CH)
-                split_store(j, rows, t, F[0, t, j, pl.ds(PAD + c * CH, CH), :])
-        return carry
-
-    for m in range(4):
-        pack(0, m)
-        ax_copy(0, m).start()
-    lax.fori_loop(0, NTL, first_split, 0)
-    for p in range(2, 4):
-        az_first(p).start()
-
     row = lax.broadcasted_iota(jnp.int32, (R, 128), 0)
     spacing = 1.0 / (NR + 1)
     radius = 1.0 + ((me * R + row).astype(F32) + 1.0) * spacing
@@ -266,8 +179,107 @@
     TB[me, 2:3, :] = SPK[0, R - 1 : R, :]
     TB[me, 3:4, :] = SPK[1, R - 1 : R, :]
     TB[me, 4:8, :] = jnp.zeros((4, 128), F32)
+    pl.semaphore_wait(barrier, n + 2)
+
+    def tile_of(p):
+        return near if p < 2 else far
+
+    def az_first(p):
+        e = p % 2
+        return pltpu.make_async_remote_copy(
+            src_ref=F.at[0, tile_of(p), pl.ds(edge_first[e] + 2, 2), pl.ds(PAD, R), :],
+            dst_ref=F.at[0, tile_of(p), pl.ds((1 - side_of[e]) * (NTL + 2), 2), pl.ds(PAD, R), :],
+            send_sem=a0_ss.at[p], recv_sem=a0_rs.at[p], device_id={"az": beside[e]},
+            device_id_type=MESH)
+
+    def az_copy(s, p):
+        return pltpu.make_async_remote_copy(
+            src_ref=YE.at[s - 1, p], dst_ref=HA.at[s - 1, p], send_sem=az_ss.at[s - 1, p],
+            recv_sem=az_rs.at[s - 1, p], device_id={"az": beside[p % 2]},
+            device_id_type=MESH)
+
+    def lh_copy(s, p):
+        return pltpu.make_async_remote_copy(
+            src_ref=LS.at[s - 1, p], dst_ref=LR.at[s - 1, p], send_sem=lh_ss.at[s - 1, p],
+            recv_sem=lh_rs.at[s - 1, p], device_id={"az": beside[p % 2]},
+            device_id_type=MESH)
+
+    def ax_copy(s, m):
+        return pltpu.make_async_remote_copy(
+            src_ref=PS.at[s, m], dst_ref=PR.at[s, m], send_sem=ax_ss.at[s, m],
+            recv_sem=ax_rs.at[s, m], device_id={"ax": other}, device_id_type=MESH)
+
+    def rad_send(buf, ss, rs, d):
+        return pltpu.make_async_remote_copy(
+            src_ref=buf.at[me], dst_ref=buf.at[me], send_sem=ss.at[d],
+            recv_sem=rs.at[me], device_id={"rad": peers[d]}, device_id_type=MESH)
+
+    def rad_recv(buf, ss, rs, d):
+        return pltpu.make_async_remote_copy(
+            src_ref=buf.at[me], dst_ref=buf.at[peers[d]], send_sem=ss.at[d],
+            recv_sem=rs.at[peers[d]], device_id={"rad": peers[d]}, device_id_type=MESH)
+
+    for j in edges:
+        for t in range(2):
+            v_copy(t, j).wait()
+    for p in range(2):
+        az_first(p).start()
+    for c in row_copies:
+        c.wait()
     for d in range(n - 1):
+        rad_send(RB0, r0_ss, r0_rs, d).start()
         rad_send(TB, t_ss, t_rs, d).start()
+
+    lane = lax.broadcasted_iota(jnp.int32, (CH, 128), 1)
+
+    def members_of(m):
+        if m is None:
+            return [x for q in range(4) for x in members_of(q)]
+        inner = [first_of[m] + i for i in range(GI)]
+        layers = ([edge_first[m], edge_first[m] + 1] if m < 2 else []) + inner
+        first = m * GI + 2 * min(m, 2)
+        return [(first + i, j) for i, j in enumerate(layers)]
+
+    def pack(s, m):
+        b = lax.rem(s, 2)
+        for c in range(R // CH):
+            acc = jnp.zeros((CH, 128), F32)
+            for i, j in members_of(m):
+                edge = F[b, near, j + 2, pl.ds(PAD + c * CH, CH), :]
+                acc = jnp.where(lane // 2 == i, pltpu.roll(edge, 2 * i + 2 * (1 - ax), 1), acc)
+            PS[s, m or 0, pl.ds(c * CH, CH), :] = acc
+
+    def unpack(s, m):
+        for c in range(R // CH):
+            rows = pl.ds(c * CH, CH)
+            x = PR[s, jnp.where(s == 0, 0, m), rows, :]
+            high = x.astype(bf).astype(F32)
+            x = jnp.where(lane < 64, high, pltpu.roll(x - high, 64, 1))
+            for i, j in members_of(m):
+                FB[j, rows, pl.ds(512, 128)] = jnp.where((lane % 64) // 2 == i, x, 0.0).astype(bf)
+
+    def split_store(j, rows, t, x):
+        high = x.astype(bf)
+        at = pl.multiple_of(t * 128, 128) if not isinstance(t, int) else t * 128
+        FB[j, rows, pl.ds(at, 128)] = high
+        FB[j, rows, pl.ds(256 + at, 128)] = (x - high.astype(F32)).astype(bf)
+
+    for j in range(2, NTL - 2):
+        for t in range(2):
+            v_copy(t, j).wait()
+
+    def first_split(j, carry):
+        for t in range(2):
+            for c in range(R // CH):
+                rows = pl.ds(c * CH, CH)
+                split_store(j, rows, t, F[0, t, j + 2, pl.ds(PAD + c * CH, CH), :])
+        return carry
+
+    pack(0, None)
+    ax_copy(0, 0).start()
+    lax.fori_loop(0, NTL, first_split, 0)
+    for p in range(2, 4):
+        az_first(p).start()
 
     def band(source, t):
         d = source - (128 * t + lax.broadcasted_iota(jnp.int32, (CH, 128), 1))
@@ -296,20 +308,14 @@
 
     for q, (dst, scale) in enumerate(((RCF, -0.5 * SCALE), (ACF, None))):
         coef_copies[q].wait()
-        moves = []
         for t in range(2):
             def convert(c, carry):
                 rows = pl.ds(pl.multiple_of(c * 8, 8), 8)
                 x = STB[q, rows, :, pl.ds(128 * t, 128)].astype(F32)
-                ST[t, rows] = x if scale is None else x * scale
+                dst[t, :, rows, :] = jnp.swapaxes(x if scale is None else x * scale, 0, 1)
                 return carry
 
             lax.fori_loop(0, R // 8, convert, 0)
-            for j in range(NTL):
-                moves.append(pltpu.make_async_copy(ST.at[t, :, j, :], dst.at[t, j], cc_s.at[t, j]))
-                moves[-1].start()
-        for c in moves:
-            c.wait()
 
     for d in range(n - 1):
         rad_recv(RB0, r0_ss, r0_rs, d).wait_recv()
@@ -319,8 +325,8 @@
     high0 = jnp.where(me < n - 1, RB0[above, 0:NTL, :], 0.0)
     for j in range(NTL):
         for t in range(2):
-            F[0, t, j, PAD - 1 : PAD, :] = low0[j : j + 1, 128 * t : 128 * t + 128]
-            F[0, t, j, PAD + R : PAD + R + 1, :] = high0[j : j + 1, 128 * t : 128 * t + 128]
+            F[0, t, j + 2, PAD - 1 : PAD, :] = low0[j : j + 1, 128 * t : 128 * t + 128]
+            F[0, t, j + 2, PAD + R : PAD + R + 1, :] = high0[j : j + 1, 128 * t : 128 * t + 128]
 
     for d in range(n - 1):
         rad_recv(TB, t_ss, t_rs, d).wait_recv()
@@ -340,9 +346,9 @@
     def right_side(b, t, j, r0, near_by, slope, curve):
         rows = pl.ds(PAD + r0, CH)
         at = pl.ds(r0, CH)
-        f = F[b, t, j, rows, :]
-        lo = F[b, t, j, pl.ds(PAD + r0 - 1, CH), :]
-        up = F[b, t, j, pl.ds(PAD + r0 + 1, CH), :]
+        f = F[b, t, j + 2, rows, :]
+        lo = F[b, t, j + 2, pl.ds(PAD + r0 - 1, CH), :]
+        up = F[b, t, j + 2, pl.ds(PAD + r0 + 1, CH), :]
         m2, m1, p1, p2 = near_by
         dt = 8.0 * (p1 - m1) - (p2 - m2)
         lt = 16.0 * (p1 + m1) - (p2 + m2)
@@ -360,42 +366,50 @@
         q[pl.ds(r0, CH), cols] = high
         q[pl.ds(R + r0, CH), cols] = (x - high.astype(F32)).astype(bf)
 
-    def axial_edges(side):
-        lhs = FB[pl.ds(edge_first[side], 2)].reshape(2 * R, 640)
-        for t in range(2):
-            SCE[side, t] = jnp.dot(lhs, BW[t], preferred_element_type=F32)
+    def stencil(dst, lhs):
+        dst[near] = jnp.dot(lhs, BW[near], preferred_element_type=F32)
+        dst[far] = jnp.dot(lhs[:, 0:512], BW[far, 0:512, :], preferred_element_type=F32)
+
+    def ax_wait(s, m):
+        if m == 0:
+            ax_copy(s, m).wait()
+        else:
+            @pl.when(s > 0)
+            def _():
+                ax_copy(s, m).wait()
+
+    def axial(s, k):
+        unpack(s, k)
+        stencil(SC, FB[pl.ds(first_of[k], GI)].reshape(GI * R, 640))
+
+    def axial_edges(k):
+        stencil(SCE.at[k], FB[pl.ds(edge_first[k], 2)].reshape(2 * R, 640))
 
     def edge_solve(s, p):
         side = p % 2
         b = lax.rem(s, 2)
         t = tile_of(p)
 
-        def layer(j, r0):
-            if j < 0:
-                return HX[p, 2 + j, pl.ds(r0, CH), :]
-            if j >= NTL:
-                return HX[p, j - NTL, pl.ds(r0, CH), :]
-            return F[b, t, j, pl.ds(PAD + r0, CH), :]
+        halo = side_of[side] * (NTL + 2)
 
         @pl.when(s == 0)
         def _():
-            az_first(p ^ 1).wait_recv()
-            az_first(p).wait_send()
+            az_first(p).wait_recv()
 
         @pl.when(s > 0)
         def _():
             for copy in (az_copy, lh_copy):
-                copy(s, p ^ 1).wait_recv()
-                copy(s, p).wait_send()
+                copy(s, p).wait_recv()
             for i in range(2):
                 cols = slice(i * 128, i * 128 + 128)
                 low = LR[s - 1, p, 0:1, cols]
                 high = LR[s - 1, p, 1:2, cols]
                 for c in range(R // CH):
                     here = pl.ds(c * CH, CH)
-                    HX[p, i, here, :] = (
+                    rows = pl.ds(PAD + c * CH, CH)
+                    F[b, t, halo + i, rows, :] = (
                         HA[s - 1, p, here, cols] - SPK[0, here, :] * low
-                        - SPK[1, here, :] * high - HX[p, i, here, :])
+                        - SPK[1, here, :] * high - F[1 - b, t, halo + i, rows, :])
 
         for i in range(2):
             j = edge_first[side] + i
@@ -403,7 +417,8 @@
                 r0 = c * CH
                 at = pl.ds(i * R + r0, CH)
                 x = right_side(
-                    b, t, j, r0, [layer(j + o, r0) for o in (-2, -1, 1, 2)],
+                    b, t, j, r0,
+                    [F[b, t, j + 2 + o, pl.ds(PAD + r0, CH), :] for o in (-2, -1, 1, 2)],
                     SCE[side, t, at, 0:128], SCE[side, t, at, 128:256])
                 put_q(QE, r0, pl.ds(i * 128, 128), x)
         y = solve(QE)
@@ -432,11 +447,11 @@
         for c in range(R // CH):
             here = pl.ds(c * CH, CH)
             rows = pl.ds(PAD + c * CH, CH)
-            x = (y_of(here) - SPK[0, here, :] * low - SPK[1, here, :] * high - F[b, t, j, rows, :])
-            F[1 - b, t, j, rows, :] = x
+            x = (y_of(here) - SPK[0, here, :] * low - SPK[1, here, :] * high - F[b, t, j + 2, rows, :])
+            F[1 - b, t, j + 2, rows, :] = x
             split_store(j, here, t, x)
-        F[1 - b, t, j, PAD - 1 : PAD, :] = low - F[b, t, j, PAD - 1 : PAD, :]
-        F[1 - b, t, j, PAD + R : PAD + R + 1, :] = high - F[b, t, j, PAD + R : PAD + R + 1, :]
+        F[1 - b, t, j + 2, PAD - 1 : PAD, :] = low - F[b, t, j + 2, PAD - 1 : PAD, :]
+        F[1 - b, t, j + 2, PAD + R : PAD + R + 1, :] = high - F[b, t, j + 2, PAD + R : PAD + R + 1, :]
 
     def edge_finish(s, p):
         b = lax.rem(s, 2)
@@ -448,6 +463,15 @@
             rad_recv(buf, ss, rs, d).wait_recv()
         low, high = ends(RBE, (s, p), 256)
 
+        @pl.when(s == 0)
+        def _():
+            az_first(p).wait_send()
+
+        @pl.when(s > 0)
+        def _():
+            az_copy(s, p).wait_send()
+            lh_copy(s, p).wait_send()
+
         @pl.when(s < STEPS - 1)
         def _():
             LS[s, p, 0:1, :] = low
@@ -459,26 +483,23 @@
             advance(b, t, edge_first[p % 2] + i,
                     lambda here: YE[s, p, here, cols], low[:, cols], high[:, cols])
 
-        @pl.when(s == STEPS - 1)
-        def _():
-            for i in range(2):
-                o_copy(t, edge_first[p % 2] + i).start()
+        for q in range(2):
+            @pl.when(jnp.logical_and(s == STEPS - 1, parity == q))
+            def _():
+                for i in range(2):
+                    o_copy(t, edge(p, q) + i).start()
 
     def inner_solve(s, k):
         b = lax.rem(s, 2)
-        lhs = FB[pl.ds(first_of[k], GI)].reshape(GI * R, 640)
-        for t in range(2):
-            SC[t] = jnp.dot(lhs, BW[t], preferred_element_type=F32)
-
         def rhs(i):
             j = first_of[k] + i
-            for t in range(2):
-                for c in range(R // CH):
+            for c in range(R // CH):
+                for t in range(2):
                     r0 = c * CH
                     at = pl.ds(pl.multiple_of(i * R + r0, CH), CH)
                     x = right_side(
                         b, t, j, r0,
-                        [F[b, t, j + o, pl.ds(PAD + r0, CH), :] for o in (-2, -1, 1, 2)],
+                        [F[b, t, j + 2 + o, pl.ds(PAD + r0, CH), :] for o in (-2, -1, 1, 2)],
                         SC[t, at, 0:128], SC[t, at, 128:256])
                     put_q(Q.at[i], r0, pl.ds(t * 128, 128), x)
 
@@ -501,56 +522,79 @@
         for d in range(n - 1):
             rad_send(RBI.at[s, k], ri_ss.at[s, k], ri_rs.at[s, k], d).start()
 
-    def inner_finish(s, k):
+    def inner_finish(s, k, then=None):
         b = lax.rem(s, 2)
         buf, ss, rs = RBI.at[s, k], ri_ss.at[s, k], ri_rs.at[s, k]
         for d in range(n - 1):
             rad_send(buf, ss, rs, d).wait_send()
+        if then is not None:
+            ax_wait(*then)
         for d in range(n - 1):
             rad_recv(buf, ss, rs, d).wait_recv()
-        for h, line in enumerate(ends(RBI, (s, k), GI * NZL)):
-            LU[h : h + 1, :] = line
-
-        def body(i, c):
+        if then is not None:
+            axial(*then)
+        low, high = ends(RBI, (s, k), GI * NZL)
+        for i in range(GI):
             for t in range(2):
-                cols = pl.ds(pl.multiple_of(i * NZL + t * 128, 128), 128)
+                cols = slice(i * NZL + t * 128, i * NZL + t * 128 + 128)
                 advance(b, t, first_of[k] + i,
                         lambda here: Y[k, i, here, pl.ds(t * 128, 128)],
-                        LU[0:1, cols], LU[1:2, cols])
-            return c
-
-        lax.fori_loop(0, GI, body, 0)
-
-        @pl.when(s < STEPS - 1)
-        def _():
-            pack(s + 1, k)
-            ax_copy(s + 1, k).start()
-
-        @pl.when(s == STEPS - 1)
-        def _():
-            for i in range(GI):
-                for t in range(2):
-                    o_copy(t, first_of[k] + i).start()
+                        low[:, cols], high[:, cols])
+
+        for q in range(2):
+            @pl.when(jnp.logical_and(s == STEPS - 1, parity == q))
+            def _():
+                for i in range(GI):
+                    for t in range(2):
+                        o_copy(t, group(k, q) + i).start()
+
+    def send_axial(s, k):
+        pack(s, k)
+        ax_copy(s, k).start()
 
     def step(s, carry):
         for k in range(4):
-            ax_copy(s, k).wait_recv()
-            unpack(s, k)
             inner_solve(s, k)
-            if k < 2:
-                axial_edges(k)
             edge_solve(s, k)
             if k == 0:
                 @pl.when(s > 0)
                 def _():
+                    inner_finish(s - 1, 3, (s, 1))
                     edge_finish(s - 1, 3)
-                    inner_finish(s - 1, 3)
+                    send_axial(s, 3)
+
+                @pl.when(s == 0)
+                def _():
+                    axial(s, 1)
+
+                axial_edges(1)
+            elif k < 3:
+                inner_finish(s, k - 1, (s, k + 1))
+                edge_finish(s, k - 1)
+
+                @pl.when(s < STEPS - 1)
+                def _():
+                    send_axial(s + 1, k - 1)
             else:
-                edge_finish(s, k - 1)
-                inner_finish(s, k - 1)
-            ax_copy(s, k).wait_send()
+                @pl.when(s < STEPS - 1)
+                def _():
+                    inner_finish(s, 2, (s + 1, 0))
+
+                @pl.when(s == STEPS - 1)
+                def _():
+                    inner_finish(s, 2)
+
+                edge_finish(s, 2)
+
+                @pl.when(s < STEPS - 1)
+                def _():
+                    send_axial(s + 1, 2)
+                    axial_edges(0)
         return carry
 
+    ax_wait(0, 0)
+    axial(0, 0)
+    axial_edges(0)
     lax.fori_loop(0, STEPS, step, 0)
     inner_finish(STEPS - 1, 3)
     edge_finish(STEPS - 1, 3)
@@ -575,10 +619,9 @@
         in_specs=[hbm, hbm, hbm, pl.BlockSpec(memory_space=pltpu.VMEM)],
         out_specs=hbm,
         scratch_shapes=[
-            pltpu.VMEM((2, 2, NTL, R + 2 * PAD, 128), F32),
+            pltpu.VMEM((2, 2, NTL + 4, R + 2 * PAD, 128), F32),
             pltpu.VMEM((NTL, R, 640), bf),
             pltpu.VMEM((S - 1, 4, R, 256), F32),
-            pltpu.VMEM((4, 2, R, 128), F32),
             pltpu.VMEM((S - 1, 4, 2, 256), F32),
             pltpu.VMEM((S - 1, 4, 2, 256), F32),
             pltpu.VMEM((4, GI, R, NZL), F32),
@@ -606,14 +649,12 @@
             pltpu.VMEM((R, 128), F32),
             pltpu.VMEM((2, R, 128), F32),
             pltpu.VMEM((2, n, 2, 128), F32),
-            pltpu.VMEM((2, GI * NZL), F32),
-            pltpu.VMEM((2, R, NTL, 128), F32),
             pltpu.VMEM((2, R, NTL, NZL), bf),
             dma((4,)), dma((4,)), dma((S - 1, 4)), dma((S - 1, 4)), dma((S - 1, 4)), dma((S - 1, 4)),
             dma((S, 4)), dma((S, 4)),
             dma((n,)), dma((n,)), dma((S, 4, n)), dma((S, 4, n)),
             dma((S, 4, n)), dma((S, 4, n)), dma((n,)), dma((n,)),
-            dma((2, NTL)), dma((2,)), dma((2,)), dma((2, NTL)), dma((2, NTL)),
+            dma((2, NTL)), dma((2,)), dma((2,)), dma((2, NTL)),
         ],
         compiler_params=pltpu.CompilerParams(
             collective_id=0, has_side_effects=True, vmem_limit_bytes=58 * 1024 * 1024),

time: 94.5 us -> 91.3 us (0.966)
  Pallas kernels: 91.3 us -> 88.1 us
    pallas_call x1, Pallas kernels: 91.3 us -> 88.1 us  [local(): pl.pallas_call(functools.partial(kernel, n, naz, R, NTL, NZL), out_shape=...]
where the time goes in v3:
time: 91.3 us; the launch traced here: 91.2 us
  Pallas kernels  88.1 us (96%)
  local copies, waits for them, and re-layouts  3.08 us (3%)
    pallas_call x1, Pallas kernels, local(): pl.pallas_call(functools.partial(kernel, n, naz, R, NTL, NZL), out_shape=...  88.1 us
    unnamed x1, local copies, waits for them, and re-layouts  3.08 us

profile of v3, /device:TPU:0, one launch (start us, length us, event | category | flops | bytes accessed | tf_op | source)
XLA Modules:
  0.0 91.2 jit_solution(12423286265811751153)
XLA Ops:
  0.0 88.1 %shard_map.46 = f32[128,16,256]{2,1,0:T(8,128)} custom-call(f32[128,16,256]{2,1,0:T(8,128)} %v.1, bf16[128,16,256]{2,1,0:T(8,128)(2,1)} %rc.1, bf16[128,16,256]{2,1,0:T(8,128)(2,1)} %ac.1, f32[1,128]{1,0:T(1,128)} %bitcast.1), custom_call_target="tpu_custom_call" | custom-call | tf_op jit(solution)/shard_map/pallas_call | solution.py:616
  88.1 3.1 %copy.6 = f32[128,16,256]{2,1,0:T(8,128)} copy(f32[128,16,256]{2,1,0:T(8,128)} %shard_map.46) | data formatting | bytes 4194304

commit v4 on v3

--- a/solution.py
+++ b/solution.py
@@ -104,6 +104,13 @@
             F.at[STEPS % 2, t, j + 2, pl.ds(PAD, R), :],
             out.at[:, j, pl.ds(pl.multiple_of(128 * t, 128), 128)], o_s.at[t, j])
 
+    barrier = pltpu.get_barrier_semaphore()
+    for p in peers:
+        pl.semaphore_signal(barrier, inc=1, device_id={"rad": p}, device_id_type=MESH)
+    for p in (left, right):
+        pl.semaphore_signal(barrier, inc=1, device_id={"az": p}, device_id_type=MESH)
+    pl.semaphore_signal(barrier, inc=1, device_id={"ax": other}, device_id_type=MESH)
+
     edges = (0, 1, NTL - 2, NTL - 1)
     for j in edges:
         for t in range(2):
@@ -121,12 +128,6 @@
     for c in coef_copies:
         c.start()
 
-    barrier = pltpu.get_barrier_semaphore()
-    for p in peers:
-        pl.semaphore_signal(barrier, inc=1, device_id={"rad": p}, device_id_type=MESH)
-    for p in (left, right):
-        pl.semaphore_signal(barrier, inc=1, device_id={"az": p}, device_id_type=MESH)
-    pl.semaphore_signal(barrier, inc=1, device_id={"ax": other}, device_id_type=MESH)
     row = lax.broadcasted_iota(jnp.int32, (R, 128), 0)
     spacing = 1.0 / (NR + 1)
     radius = 1.0 + ((me * R + row).astype(F32) + 1.0) * spacing
@@ -222,7 +223,7 @@
     for j in edges:
         for t in range(2):
             v_copy(t, j).wait()
-    for p in range(2):
+    for p in range(4):
         az_first(p).start()
     for c in row_copies:
         c.wait()
@@ -278,8 +279,6 @@
     pack(0, None)
     ax_copy(0, 0).start()
     lax.fori_loop(0, NTL, first_split, 0)
-    for p in range(2, 4):
-        az_first(p).start()
 
     def band(source, t):
         d = source - (128 * t + lax.broadcasted_iota(jnp.int32, (CH, 128), 1))
@@ -559,8 +558,8 @@
             if k == 0:
                 @pl.when(s > 0)
                 def _():
+                    edge_finish(s - 1, 3)
                     inner_finish(s - 1, 3, (s, 1))
-                    edge_finish(s - 1, 3)
                     send_axial(s, 3)
 
                 @pl.when(s == 0)
@@ -569,8 +568,8 @@
 
                 axial_edges(1)
             elif k < 3:
+                edge_finish(s, k - 1)
                 inner_finish(s, k - 1, (s, k + 1))
-                edge_finish(s, k - 1)
 
                 @pl.when(s < STEPS - 1)
                 def _():

time: 91.3 us -> 91.1 us (level)
  no operation moved by 1% of the time
where the time goes in v4:
time: 91.1 us; the launch traced here: 91 us
  Pallas kernels  87.9 us (96%)
  local copies, waits for them, and re-layouts  3.08 us (3%)
    pallas_call x1, Pallas kernels, local(): pl.pallas_call(functools.partial(kernel, n, naz, R, NTL, NZL), out_shape=...  87.9 us
    unnamed x1, local copies, waits for them, and re-layouts  3.08 us

profile of v4, /device:TPU:0, one launch (start us, length us, event | category | flops | bytes accessed | tf_op | source)
XLA Modules:
  0.0 91.0 jit_solution(17415546955372764755)
XLA Ops:
  0.0 87.9 %shard_map.46 = f32[128,16,256]{2,1,0:T(8,128)} custom-call(f32[128,16,256]{2,1,0:T(8,128)} %v.1, bf16[128,16,256]{2,1,0:T(8,128)(2,1)} %rc.1, bf16[128,16,256]{2,1,0:T(8,128)(2,1)} %ac.1, f32[1,128]{1,0:T(1,128)} %bitcast.1), custom_call_target="tpu_custom_call" | custom-call | tf_op jit(solution)/shard_map/pallas_call | solution.py:615
  87.9 3.1 %copy.6 = f32[128,16,256]{2,1,0:T(8,128)} copy(f32[128,16,256]{2,1,0:T(8,128)} %shard_map.46) | data formatting | bytes 4194304

commit v5 on v4

--- a/solution.py
+++ b/solution.py
@@ -422,14 +422,15 @@
                 put_q(QE, r0, pl.ds(i * 128, 128), x)
         y = solve(QE)
         YE[s, p] = y
+
+        @pl.when(s < STEPS - 1)
+        def _():
+            az_copy(s + 1, p).start()
+
         RBE[s, p, me, 0:1, :] = y[0:1, :]
         RBE[s, p, me, 1:2, :] = y[R - 1 : R, :]
         for d in range(n - 1):
             rad_send(RBE.at[s, p], re_ss.at[s, p], re_rs.at[s, p], d).start()
-
-        @pl.when(s < STEPS - 1)
-        def _():
-            az_copy(s + 1, p).start()
 
     def ends(buf, idx, width):
         res = []

time: 91.1 us -> 91.1 us (level)
  no operation moved by 1% of the time
where the time goes in v5:
time: 91.1 us; the launch traced here: 91 us
  Pallas kernels  87.9 us (96%)
  local copies, waits for them, and re-layouts  3.08 us (3%)
    pallas_call x1, Pallas kernels, local(): pl.pallas_call(functools.partial(kernel, n, naz, R, NTL, NZL), out_shape=...  87.9 us
    unnamed x1, local copies, waits for them, and re-layouts  3.08 us

profile of v5, /device:TPU:0, one launch (start us, length us, event | category | flops | bytes accessed | tf_op | source)
XLA Modules:
  0.0 91.0 jit_solution(18247949418090303512)
XLA Ops:
  0.0 87.9 %shard_map.46 = f32[128,16,256]{2,1,0:T(8,128)} custom-call(f32[128,16,256]{2,1,0:T(8,128)} %v.1, bf16[128,16,256]{2,1,0:T(8,128)(2,1)} %rc.1, bf16[128,16,256]{2,1,0:T(8,128)(2,1)} %ac.1, f32[1,128]{1,0:T(1,128)} %bitcast.1), custom_call_target="tpu_custom_call" | custom-call | tf_op jit(solution)/shard_map/pallas_call | solution.py:616
  87.9 3.1 %copy.6 = f32[128,16,256]{2,1,0:T(8,128)} copy(f32[128,16,256]{2,1,0:T(8,128)} %shard_map.46) | data formatting | bytes 4194304
